TPU v7x, 256 devices: a whole 4x4x8 slice. The times are simulated.
256 devices in a mesh: ctx: 32 (over x, z), tp: 8 (over y, core).
Axes of the slice: x: 4, y: 4, z: 8, core: 2. Of those that a mesh axis runs over, the one named last changes fastest.
Arguments:
- moe_input: bfloat16 [4096, 6400], P('ctx', 'tp'), may hold values from -6 to 6
- out_grad: bfloat16 [4096, 6400], P('ctx', 'tp'), may hold values from -6 to 6
- route_prob: float32 [4096, 2], P('ctx'), may hold values from 0.2 to 1
- route_ids: int32 [4096, 2], P('ctx'), may hold values from 0 to 31, as said below
- route_counts: int32 [32, 32], P('ctx'), may hold values from 0 to 16, as said below
- w_gate: bfloat16 [32, 6400, 1536], P('ctx', 'tp'), may hold values from -0.078125 to 0.078125
- w_up: bfloat16 [32, 6400, 1536], P('ctx', 'tp'), may hold values from -0.078125 to 0.078125
- w_down: bfloat16 [32, 1536, 6400], P('ctx', None, 'tp'), may hold values from -0.15625 to 0.15625
- out_weight: bfloat16 [6400, 8192], P('ctx', 'tp'), may hold values from -0.078125 to 0.078125
- ssd_input: bfloat16 [4096, 8192], P('ctx', 'tp'), may hold values from -0.19921875 to 0.19921875
- input_map: bfloat16 [4096, 1024], P('ctx', 'tp'), may hold values from -0.29882812 to 0.29882812
- output_map: bfloat16 [4096, 1024], P('ctx', 'tp'), may hold values from -0.29882812 to 0.29882812
- log_decay: float32 [4096, 128], P('ctx', 'tp'), may hold values from -2.2 to 0
Outputs:
- input_grad: bfloat16 [4096, 6400], P('ctx', 'tp')
- scan_grad: bfloat16 [4096, 8192], P('ctx', 'tp')
- in_map_grad: float32 [4096, 1024], P('ctx', 'tp')
- out_map_grad: float32 [4096, 1024], P('ctx', 'tp')
Inputs may be any that keep to these rules, and one draw needn't show every extreme that they name: `route_ids`: each row names 2 different experts. Among the 128 rows of one device (rows c * 128 to (c + 1) * 128 - 1) no expert is named more than 16 times, and in the rows of every device some expert is named exactly 16 times. route_counts[c, e] is the most entries among rows c * 128 to (c + 1) * 128 - 1 of route_ids that expert e accepts; it never exceeds the number of those rows that name e.
All inputs are finite; a program needn't handle non-finite values.
Results may differ from a plain program's by a relative error of at most 0.027.
Values may be sent and summed in bfloat16 or wider, within the bound.
A program may use at most 128 MiB of HBM per device.

v0:
```python
import jax
import jax.numpy as jnp
from jax import lax
from jax.sharding import PartitionSpec as P

highest = lax.Precision.HIGHEST


def entering(x, axis, join, neutral, backward):
    count = lax.axis_size(axis)
    place = lax.axis_index(axis)
    ahead = count - 1 - place if backward else place
    gathered = jax.tree.map(
        lambda a, kind: lax.all_gather(a.astype(kind), axis), x, (jnp.bfloat16, jnp.bfloat16)
    )
    state = jax.tree.map(lambda a, e: jnp.zeros_like(a) + jnp.asarray(e, a.dtype), x, neutral)

    def one(hop, state):
        source = count - 1 - hop if backward else hop
        return join(
            state,
            jax.tree.map(
                lambda a, own: lax.dynamic_index_in_dim(a, source, 0, False).astype(own.dtype),
                gathered,
                x,
            ),
        )

    return lax.fori_loop(0, ahead, one, state)


def swiglu_back(pre_gate, pre_up, back):
    sigma = jax.nn.sigmoid(pre_gate)
    gate_grad = back * pre_up * sigma * (1.0 + pre_gate * (1.0 - sigma))
    up_grad = back * pre_gate * sigma
    return (gate_grad.astype(jnp.bfloat16), up_grad.astype(jnp.bfloat16))


def decay_kernel(running):
    count = running.shape[0]
    later = (jnp.arange(count)[:, None] >= jnp.arange(count)[None, :])[None, :, :]
    spread = running.T[:, :, None] - running.T[:, None, :]
    return jnp.where(later, jnp.exp(jnp.where(later, spread, 0.0)), 0.0)


def local_terms(inputs, grads, in_map, out_map, running):
    kernel = decay_kernel(running)
    inner = jnp.einsum("thp,shp->hts", grads, inputs, precision=highest)
    weighted = kernel * inner
    affinity = jnp.einsum("tn,sn->ts", out_map, in_map, precision=highest)
    scan_part = jnp.einsum("hts,ts,thp->shp", kernel, affinity, grads, precision=highest)
    in_part = jnp.einsum("hts,tn->sn", weighted, out_map, precision=highest)
    out_part = jnp.einsum("hts,sn->tn", weighted, in_map, precision=highest)
    return (scan_part, in_part, out_part)


def chain_combine(earlier, later):
    return (earlier[0] * later[0], later[1] + later[0][:, None, None] * earlier[1])


def body(
    moe_input,
    out_grad,
    route_prob,
    route_ids,
    route_counts,
    w_gate,
    w_up,
    w_down,
    out_weight,
    ssd_input,
    input_map,
    output_map,
    log_decay,
):
    tok_count, width = moe_input.shape
    top_count = route_ids.shape[1]
    expert_count = route_counts.shape[1]
    source_count = lax.axis_size("ctx")
    capacity = 2 * tok_count * top_count // expert_count
    heads = log_decay.shape[1]
    head_cols = ssd_input.shape[1]
    head_size = head_cols // heads
    inputs = ssd_input.astype(jnp.float32).reshape(tok_count, heads, head_size)
    in_map = input_map.astype(jnp.float32)
    out_map = output_map.astype(jnp.float32)
    running = jnp.cumsum(log_decay, axis=0)
    block_total = running[-1]
    tail = jnp.exp(block_total[None, :] - running)
    carry_decay = jnp.exp(block_total)
    state_local = jnp.einsum("sh,shp,sn->hpn", tail, inputs, in_map, precision=highest)
    identity = (jnp.ones_like(carry_decay), jnp.zeros_like(state_local))
    state_before = entering((carry_decay, state_local), "ctx", chain_combine, identity, False)[1]
    flat_ids = route_ids.reshape(-1)
    member = (flat_ids[:, None] == jnp.arange(expert_count, dtype=jnp.int32)[None, :]).astype(
        jnp.int32
    )
    entry_rank = jnp.sum((jnp.cumsum(member, axis=0) - member) * member, axis=1)
    allowed = jnp.sum(member * route_counts, axis=1)
    slot_index = jnp.where(
        entry_rank < allowed, flat_ids * capacity + entry_rank, expert_count * capacity
    )
    entry_rows = jnp.repeat(moe_input, top_count, axis=0)
    scaled = (
        (route_prob[:, :, None] * out_grad[:, None, :].astype(jnp.float32))
        .astype(jnp.bfloat16)
        .reshape(tok_count * top_count, width)
    )
    send_rows = (
        jnp.zeros((expert_count * capacity, width), jnp.bfloat16)
        .at[slot_index]
        .set(entry_rows, mode="drop")
        .reshape(source_count, -1, width)
    )
    send_grads = (
        jnp.zeros((expert_count * capacity, width), jnp.bfloat16)
        .at[slot_index]
        .set(scaled, mode="drop")
        .reshape(source_count, -1, width)
    )
    gate_local = w_gate[0]
    up_local = w_up[0]
    down_local = w_down[0]
    rows_in = lax.all_to_all(send_rows, "ctx", split_axis=0, concat_axis=0, tiled=True)
    grads_in = lax.all_to_all(send_grads, "ctx", split_axis=0, concat_axis=0, tiled=True)
    sources, items, cols = rows_in.shape
    flat_rows = rows_in.reshape(sources * items, cols)
    flat_grads = grads_in.reshape(sources * items, cols)
    gate_part = jnp.dot(flat_rows, gate_local, preferred_element_type=jnp.float32)
    up_part = jnp.dot(flat_rows, up_local, preferred_element_type=jnp.float32)
    back_part = jnp.einsum("rd,fd->rf", flat_grads, down_local, preferred_element_type=jnp.float32)
    pre_gate = lax.psum(gate_part.astype(jnp.bfloat16), "tp").astype(jnp.float32)
    pre_up = lax.psum(up_part.astype(jnp.bfloat16), "tp").astype(jnp.float32)
    back = lax.psum(back_part.astype(jnp.bfloat16), "tp").astype(jnp.float32)
    gate_grad, up_grad = swiglu_back(pre_gate, pre_up, back)
    entry_grad = jnp.einsum("rf,df->rd", gate_grad, gate_local, preferred_element_type=jnp.float32)
    entry_grad = entry_grad + jnp.einsum(
        "rf,df->rd", up_grad, up_local, preferred_element_type=jnp.float32
    )
    returned = entry_grad.astype(jnp.bfloat16).reshape(sources, items, cols)
    returned = lax.all_to_all(returned, "ctx", split_axis=0, concat_axis=0, tiled=True)
    back_flat = returned.reshape(-1, width)
    collected = jnp.take(back_flat, slot_index, axis=0, mode="fill", fill_value=0)
    summed = jnp.sum(collected.astype(jnp.float32).reshape(tok_count, top_count, width), axis=1)
    input_grad = (out_grad.astype(jnp.float32) + summed).astype(jnp.bfloat16)
    full_grad = lax.all_gather(input_grad, "tp", axis=1, tiled=True)
    head_sum = jnp.dot(
        full_grad,
        lax.all_gather(out_weight, "ctx", axis=0, tiled=True),
        preferred_element_type=jnp.float32,
    )
    head_grad = head_sum.astype(jnp.bfloat16)
    grads = head_grad.astype(jnp.float32).reshape(tok_count, heads, head_size)
    grad_local = jnp.einsum("th,thp,tn->hpn", jnp.exp(running), grads, out_map, precision=highest)
    grad_after = entering((carry_decay, grad_local), "ctx", chain_combine, identity, True)[1]
    scan_intra, in_intra, out_intra = local_terms(inputs, grads, in_map, out_map, running)
    out_map_grad = out_intra + jnp.einsum(
        "th,thp,hpn->tn", jnp.exp(running), grads, state_before, precision=highest
    )
    in_map_grad = in_intra + jnp.einsum(
        "sh,shp,hpn->sn", tail, inputs, grad_after, precision=highest
    )
    scan_part = scan_intra + jnp.einsum(
        "sh,hpn,sn->shp", tail, grad_after, in_map, precision=highest
    )
    scan_grad = scan_part.reshape(tok_count, head_cols).astype(jnp.bfloat16)
    return (input_grad, scan_grad, in_map_grad, out_map_grad)


def solution(mesh):
    in_specs = (
        P("ctx", "tp"),
        P("ctx", "tp"),
        P("ctx", None),
        P("ctx", None),
        P("ctx", None),
        P("ctx", "tp", None),
        P("ctx", "tp", None),
        P("ctx", None, "tp"),
        P("ctx", "tp"),
        P("ctx", "tp"),
        P("ctx", "tp"),
        P("ctx", "tp"),
        P("ctx", "tp"),
    )
    out_specs = (P("ctx", "tp"), P("ctx", "tp"), P("ctx", "tp"), P("ctx", "tp"))
    return jax.shard_map(body, mesh=mesh, in_specs=in_specs, out_specs=out_specs, check_vma=False)
```

profile of v0, /device:TPU:1, one launch (start us, length us, event | category | flops | bytes accessed | tf_op | source)
XLA Modules:
  0.0 624.1 jit_solution(5866926999444945971)
XLA Ops:
  11.2 2.7 scatter_custom_fusion.1
  13.9 12.1 %all-to-all-start.1 = ((bf16[32,16,800]{2,1,0:T(8,128)(2,1)}), bf16[32,16,800]{2,1,0:T(8,128)(2,1)}, u32[]{:S(2)}, u32[]{:S(2)}) async-start(bf16[32,16,800]{2,1,0:T(8,128)(2,1)} %bitcast.12), calls=%async_computation.1 | async-start | bytes 1835008 | tf_op jit(solution)/shard_map/all_to_all | solution.py:124
  26.9 1.2 mul.113
  28.1 1.8 mul.114
  30.2 2.7 scatter_custom_fusion
  32.9 15.0 %all-to-all-done.1 = bf16[32,16,800]{2,1,0:T(8,128)(2,1)} async-done(((bf16[32,16,800]{2,1,0:T(8,128)(2,1)}), bf16[32,16,800]{2,1,0:T(8,128)(2,1)}, u32[]{:S(2)}, u32[]{:S(2)}) %all-to-all-start.1) | async-done | bytes 819232 | tf_op jit(solution)/shard_map/all_to_all | solution.py:124
  48.0 8.5 %all-to-all-start = ((bf16[32,16,800]{2,1,0:T(8,128)(2,1)}), bf16[32,16,800]{2,1,0:T(8,128)(2,1)S(1)}, u32[]{:S(2)}, u32[]{:S(2)}) async-start(bf16[32,16,800]{2,1,0:T(8,128)(2,1)} %bitcast.9), calls=%async_computation | async-start | bytes 1835008 | tf_op jit(solution)/shard_map/all_to_all | solution.py:125
  56.7 4.9 convolution_convert_fusion
  61.6 4.1 convolution_convert_fusion.1
  65.7 12.7 %all-to-all-done = bf16[32,16,800]{2,1,0:T(8,128)(2,1)S(1)} async-done(((bf16[32,16,800]{2,1,0:T(8,128)(2,1)}), bf16[32,16,800]{2,1,0:T(8,128)(2,1)S(1)}, u32[]{:S(2)}, u32[]{:S(2)}) %all-to-all-start) | async-done | bytes 819232 | tf_op jit(solution)/shard_map/all_to_all | solution.py:125
  78.4 4.7 convolution_convert_fusion.2
  83.1 79.2 %all-reduce.3.cloned.1.call-done = (bf16[512,1536]{1,0:T(8,128)(2,1)}, bf16[512,1536]{1,0:T(8,128)(2,1)}, bf16[512,1536]{1,0:T(8,128)(2,1)}) async-done(((bf16[512,1536]{1,0:T(8,128)(2,1)}, bf16[512,1536]{1,0:T(8,128)(2,1)}, bf16[512,1536]{1,0:T(8,128)(2,1)}), (bf16[512,1536]{1,0:T(8,128)(2,1)}, bf16[512,1536]{1,0:T(8,128)(2,1)}, bf16[512,1536]{1,0:T(8,128)(2,1)})) %all-reduce.3.cloned.1.call-update) | async-done | bytes 4718608 | tf_op jit(solution)/shard_map/psum | solution.py:132
  162.4 3.6 fusion.12
  166.4 1.8 add_convert_fusion
  168.2 1.3 copy.77
  169.5 9.5 %all-to-all-start.2 = ((bf16[32,16,800]{2,1,0:T(8,128)(2,1)}), bf16[32,16,800]{2,1,0:T(8,128)(2,1)S(1)}, u32[]{:S(2)}, u32[]{:S(2)}) async-start(bf16[32,16,800]{2,1,0:T(8,128)(2,1)} %bitcast.122), calls=%async_computation.2 | async-start | bytes 1835008 | tf_op jit(solution)/shard_map/all_to_all | solution.py:141
  180.9 19.4 %all-to-all-done.2 = bf16[32,16,800]{2,1,0:T(8,128)(2,1)S(1)} async-done(((bf16[32,16,800]{2,1,0:T(8,128)(2,1)}), bf16[32,16,800]{2,1,0:T(8,128)(2,1)S(1)}, u32[]{:S(2)}, u32[]{:S(2)}) %all-to-all-start.2) | async-done | bytes 819232 | tf_op jit(solution)/shard_map/all_to_all | solution.py:141
  200.3 2.0 gather_fusion
  202.2 1.2 gather.7
  203.5 1.3 convert_reduce_fusion
  209.5 25.6 %all-gather.8.cloned.1.call-done = bf16[128,6400]{0,1:T(8,128)(2,1)} async-done(((bf16[128,800]{0,1:T(8,128)(2,1)}), bf16[128,6400]{0,1:T(8,128)(2,1)}) %all-gather.8.cloned.1.call-update) | async-done | bytes 1638416 | tf_op jit(solution)/shard_map/all_gather | solution.py:146
  235.0 124.3 %all-gather.10.cloned.1.call-done = bf16[6400,1024]{1,0:T(8,128)(2,1)} async-done(((bf16[200,1024]{1,0:T(8,128)(2,1)}), bf16[6400,1024]{1,0:T(8,128)(2,1)}) %all-gather.10.cloned.1.call-update) | async-done | bytes 13107216 | tf_op jit(solution)/shard_map/all_gather | solution.py:149
  359.3 7.1 %convolution_convert_fusion.3 = bf16[128,1024]{1,0:T(8,128)(2,1)S(1)} fusion(bf16[128,6400]{0,1:T(8,128)(2,1)} %all-gather.8.cloned.1.call-done, bf16[6400,1024]{1,0:T(8,128)(2,1)} %all-gather.10.cloned.1.call-done), kind=kOutput, calls=%fused_computation.37 | convolution fusion | flops 1677852672 | bytes 15007744 | tf_op jit(solution)/shard_map/dot_general | solution.py:147
  367.7 32.3 %all-gather.2 = bf16[32,1,16]{2,1,0:T(2,128)(2,1)S(1)} all-gather(bf16[1,1,16]{2,1,0:T(2,128)(2,1)S(1)} %get-tuple-element.208), channel_id=1, replica_groups=mesh['ctx'=32,'tp'=8] {'ctx'}, dimensions={0}, use_global_device_ids=true | all-gather | bytes 1056 | tf_op jit(solution)/shard_map/all_gather | solution.py:14
  402.7 54.2 %all-gather.14.cloned.1.call-done = bf16[512,64,128]{2,1,0:T(8,128)(2,1)} async-done(((bf16[16,64,128]{2,1,0:T(8,128)(2,1)}), bf16[512,64,128]{2,1,0:T(8,128)(2,1)}) %all-gather.14.cloned.1.call-update) | async-done | bytes 8388624 | tf_op jit(solution)/shard_map/all_gather | solution.py:14
  458.0 1.3 fusion.22
  460.8 94.4 %all-gather.12.cloned.1.call-done = bf16[512,64,128]{2,1,0:T(8,128)(2,1)} async-done(((bf16[16,64,128]{2,1,0:T(8,128)(2,1)}), bf16[512,64,128]{2,1,0:T(8,128)(2,1)}) %all-gather.12.cloned.1.call-update) | async-done | bytes 8388624 | tf_op jit(solution)/shard_map/all_gather | solution.py:14
  555.3 56.6 %while.26 = (s32[]{:T(128)}, f32[16,64,128]{2,1,0:T(8,128)S(1)}, s32[]{:T(128)}, bf16[32,16,64,128]{3,2,1,0:T(8,128)(2,1)}, bf16[32,16]{1,0:T(8,128)(2,1)}, /*index=5*/s32[]{:T(128)}, s32[]{:T(128)}, s32[]{:T(128)}, s32[]{:T(128)}) while((s32[]{:T(128)}, f32[16,64,128]{2,1,0:T(8,128)S(1)}, s32[]{:T(128)}, ...), condition=%wide.region_12.13_spmd, body=%wide.region_11.12_spmd.sunk | while | flops 393238 | bytes 1311027 | solution.py:29
  556.0 1.1 convert_add_fusion.4
  557.8 1.1 convert_add_fusion.4
  613.3 1.7 convolution_add_fusion.1
  615.0 1.7 fusion.25
  (146 shorter events, 74.3 us)
Async XLA Ops:
  7.2 54.4 %copy-start = (bf16[1,800,1536]{2,1,0:T(8,128)(2,1)S(1)}, bf16[1,800,1536]{2,1,0:T(8,128)(2,1)}, u32[]{:S(2)}) copy-start(bf16[1,800,1536]{2,1,0:T(8,128)(2,1)} %param.23) | copy-start | bytes 7372804
  7.2 3.9 copy-start.10
  11.1 14.9 %copy-start.6 = (bf16[128,800]{0,1:T(8,128)(2,1)S(1)}, bf16[128,800]{0,1:T(8,128)(2,1)}, u32[]{:S(2)}) copy-start(bf16[128,800]{0,1:T(8,128)(2,1)} %param.18) | copy-start | bytes 614404
  13.9 16.0 %copy-start.9 = (f32[128,2]{0,1:T(2,128)S(1)}, f32[128,2]{0,1:T(2,128)}, u32[]{:S(2)}) copy-start(f32[128,2]{0,1:T(2,128)} %param.19) | copy-start | bytes 3076
  13.9 34.1 %all-to-all-start.1 = ((bf16[32,16,800]{2,1,0:T(8,128)(2,1)}), bf16[32,16,800]{2,1,0:T(8,128)(2,1)}, u32[]{:S(2)}, u32[]{:S(2)}) async-start(bf16[32,16,800]{2,1,0:T(8,128)(2,1)} %bitcast.12), calls=%async_computation.1 | async-start | bytes 1835008 | tf_op jit(solution)/shard_map/all_to_all | solution.py:124
  26.2 0.7 copy-start.1
  48.0 30.4 %all-to-all-start = ((bf16[32,16,800]{2,1,0:T(8,128)(2,1)}), bf16[32,16,800]{2,1,0:T(8,128)(2,1)S(1)}, u32[]{:S(2)}, u32[]{:S(2)}) async-start(bf16[32,16,800]{2,1,0:T(8,128)(2,1)} %bitcast.9), calls=%async_computation | async-start | bytes 1835008 | tf_op jit(solution)/shard_map/all_to_all | solution.py:125
  56.4 105.9 %all-reduce.3.cloned.1.call-start = ((), (), s32[]{:S(2)}) async-start(), calls=%async_computation.7 | async-start | bytes 9437184 | tf_op jit(solution)/shard_map/psum | solution.py:132
  162.3 3.6 copy-start.11
  162.4 3.6 copy-start.12
  162.4 3.6 copy-start.13
  162.4 4.0 copy-start.14
  169.5 30.8 %all-to-all-start.2 = ((bf16[32,16,800]{2,1,0:T(8,128)(2,1)}), bf16[32,16,800]{2,1,0:T(8,128)(2,1)S(1)}, u32[]{:S(2)}, u32[]{:S(2)}) async-start(bf16[32,16,800]{2,1,0:T(8,128)(2,1)} %bitcast.122), calls=%async_computation.2 | async-start | bytes 1835008 | tf_op jit(solution)/shard_map/all_to_all | solution.py:141
  179.0 56.0 %all-gather.8.cloned.1.call-start = ((), (), s32[]{:S(2)}) async-start(), calls=%async_computation.3 | async-start | bytes 1843200 | tf_op jit(solution)/shard_map/all_gather | solution.py:146
  202.2 5.2 copy-start.7
  202.2 5.6 copy-start.5
  202.2 5.8 copy-start.2
  206.6 152.6 %all-gather.10.cloned.1.call-start = ((), (), s32[]{:S(2)}) async-start(), calls=%async_computation.4 | async-start | bytes 13516800 | tf_op jit(solution)/shard_map/all_gather | solution.py:149
  207.4 249.6 %all-gather.14.cloned.1.call-start = ((), (), s32[]{:S(2)}) async-start(), calls=%async_computation.6 | async-start | bytes 8650752 | tf_op jit(solution)/shard_map/all_gather | solution.py:14
  209.1 346.1 %all-gather.12.cloned.1.call-start = ((), (), s32[]{:S(2)}) async-start(), calls=%async_computation.5 | async-start | bytes 8650752 | tf_op jit(solution)/shard_map/all_gather | solution.py:14
  209.5 157.1 %copy-start.3 = (bf16[128,128]{1,0:T(8,128)(2,1)S(1)}, bf16[128,128]{1,0:T(8,128)(2,1)}, u32[]{:S(2)}) copy-start(bf16[128,128]{1,0:T(8,128)(2,1)} %param.28) | copy-start | bytes 98308
  459.3 0.6 copy-start.4
  555.2 59.7 %copy-start.8 = (f32[16,128]{1,0:T(8,128)S(1)}, f32[16,128]{1,0:T(8,128)}, u32[]{:S(2)}) copy-start(f32[16,128]{1,0:T(8,128)} %copy.79) | copy-start | bytes 24580
Sparse Core Ops, SparseCore 0:
  83.3 79.0 all-reduce.2
  206.8 28.2 all-gather.7
  237.6 121.6 all-gather.9
  361.7 95.1 all-gather.13
  459.9 95.2 all-gather.11
where the time goes:
time: 627 us; the launch traced here: 624 us
  waiting for transfers between devices  426 us (68%)
  other arithmetic  63.1 us (10%)
  matrix products  37.2 us (6%)
  blocking collectives  32.3 us (5%)
  starting transfers between devices  30.7 us (5%)
  local copies, waits for them, and re-layouts  20.1 us (3%)
  between operations  14.1 us (2%)
    all_gather x2, waiting for transfers between devices, entering(): lax.all_gather(a.astype(kind), axis)  149 us
    all_gather x1, waiting for transfers between devices, body(): lax.all_gather(out_weight, 'ctx', axis=0, tiled=True)  124 us
    psum x1, waiting for transfers between devices, body(): lax.psum(gate_part.astype(jnp.bfloat16), 'tp').astype(jnp.float32)  79.2 us
    add x31, other arithmetic, chain_combine(): later[1] + later[0][:, None, None] * earlier[1]  34.2 us
    all_gather x1, blocking collectives, entering(): lax.all_gather(a.astype(kind), axis)  32.3 us
    all_gather x1, waiting for transfers between devices, body(): full_grad = lax.all_gather(input_grad, 'tp', axis=1, tiled=True)  25.6 us
    convert_element_type x31, other arithmetic, one(): lax.dynamic_index_in_dim(a, source, 0, False).astype(own.dtype)  21.4 us
    all_to_all x1, waiting for transfers between devices, body(): lax.all_to_all(returned, 'ctx', split_axis=0, concat_axis=0, tiled=True)  19.4 us
  transfers between devices with their start and end apart: 8, of which 8 were waited for; matrix products, arithmetic and copies ran while one was open for 5% of the time, Pallas kernels for 0%

commit v1 on v0

v1 whole, which is shorter than its diff:
```python
import functools

import jax
import jax.numpy as jnp
from jax import lax
from jax.experimental import pallas as pl
from jax.experimental.pallas import tpu as pltpu
from jax.sharding import PartitionSpec as P

MESH = pl.DeviceIdType.MESH
HIGHEST = lax.Precision.HIGHEST
bf16, f32, i32 = jnp.bfloat16, jnp.float32, jnp.int32
VMEM = pl.BlockSpec(memory_space=pltpu.VMEM)
ANY = pl.BlockSpec(memory_space=pl.ANY)
DMA = pltpu.SemaphoreType.DMA


def mm(a, b, ca=1, cb=0, precision=None):
    return lax.dot_general(
        a, b, (((ca,), (cb,)), ((), ())), precision=precision, preferred_element_type=f32
    )


def remote(src, dst, send, recv, axis, place):
    return pltpu.make_async_remote_copy(
        src_ref=src,
        dst_ref=dst,
        send_sem=send,
        recv_sem=recv,
        device_id={axis: place},
        device_id_type=MESH,
    )


def hello_ctx(n, me):
    barrier = pltpu.get_barrier_semaphore()

    def one(i, _):
        pl.semaphore_signal(
            barrier, inc=1, device_id={"ctx": lax.rem(me + i, n)}, device_id_type=MESH
        )
        return 0

    lax.fori_loop(1, n, one, 0)


def hello_tp(places):
    barrier = pltpu.get_barrier_semaphore()
    for place in places:
        pl.semaphore_signal(barrier, inc=1, device_id={"tp": place}, device_id_type=MESH)


def exchange(n, me, src, dst, send, recv, act):
    def one(i, _):
        to = lax.rem(me + i, n)
        back = lax.rem(me - i + n, n)
        if act == "start":
            remote(src.at[to], dst.at[me], send.at[i], recv.at[i], "ctx", to).start()
        else:
            copy = remote(src.at[to], dst.at[back], send.at[i], recv.at[i], "ctx", to)
            copy.wait_recv()
            copy.wait_send()
        return 0

    lax.fori_loop(1, n, one, 0)


def spread(columns, total):
    heads = columns.shape[1]
    size = total // heads
    put = lax.broadcasted_iota(i32, (heads, total), 1) // size == lax.broadcasted_iota(
        i32, (heads, total), 0
    )
    return mm(columns, put.astype(f32), precision=HIGHEST)


def scan_states(n, me, loc, out, totals, rows_per_head, backward):
    head = me * loc.shape[1] // rows_per_head
    lane = lax.broadcasted_iota(i32, totals.shape, 2)
    decay = jnp.exp(jnp.sum(jnp.where(lane == head, totals[...], 0.0), axis=2, keepdims=True))
    state = jnp.zeros(loc.shape[1:], f32)
    order = range(n - 1, -1, -1) if backward else range(n)
    for c in order:
        out[c] = state.astype(bf16)
        state = decay[c, 0:1, :] * state + loc[c].astype(f32)


def dispatch_kernel(
    n,
    x_ref,
    g_ref,
    ids_ref,
    prob_ref,
    counts_ref,
    u_ref,
    b_ref,
    c_ref,
    ld_ref,
    rows_ref,
    grads_ref,
    pick_ref,
    er_ref,
    tail_ref,
    ut_ref,
    decay_ref,
    mix_ref,
    before_ref,
    tot_ref,
    send_x,
    send_g,
    st_send,
    st_recv,
    back_send,
    tot_send,
    sem_x,
    sem_g,
    sem_s,
    sem_t,
    sem_b,
):
    me = lax.axis_index("ctx")
    hello_ctx(n, me)
    tok = x_ref.shape[0]
    experts = counts_ref.shape[1]
    cap = rows_ref.shape[1]
    slots = experts * cap

    ids = ids_ref[...]
    names = lax.broadcasted_iota(i32, (tok, experts), 1)
    m0 = ids[:, 0:1] == names
    m1 = ids[:, 1:2] == names
    member = jnp.where(m0, 1.0, 0.0) + jnp.where(m1, 1.0, 0.0)
    t_row = lax.broadcasted_iota(i32, (tok, tok), 0)
    t_col = lax.broadcasted_iota(i32, (tok, tok), 1)
    rank = mm(jnp.where(t_row > t_col, 1.0, 0.0).astype(bf16), member.astype(bf16))
    slot = jnp.where(
        rank < counts_ref[...].astype(f32), rank + (names * cap).astype(f32), -1.0
    )
    place = lax.broadcasted_iota(i32, (tok, slots), 1).astype(f32)
    p0 = jnp.where(place == jnp.sum(jnp.where(m0, slot, 0.0), 1, keepdims=True), 1.0, 0.0)
    p1 = jnp.where(place == jnp.sum(jnp.where(m1, slot, 0.0), 1, keepdims=True), 1.0, 0.0)
    both = (p0 + p1).astype(bf16)
    pick_ref[...] = both
    send_x[...] = mm(both, x_ref[...], 0, 0).astype(bf16).reshape(send_x.shape)
    grad = g_ref[...].astype(f32)
    prob = prob_ref[...]
    scaled = jnp.concatenate(
        [(prob[:, 0:1] * grad).astype(bf16), (prob[:, 1:2] * grad).astype(bf16)], axis=0
    )
    pair = jnp.concatenate([p0.astype(bf16), p1.astype(bf16)], axis=0)

    pl.semaphore_wait(pltpu.get_barrier_semaphore(), n - 1)
    exchange(n, me, send_x, rows_ref, sem_x.at[0], sem_x.at[1], "start")
    send_g[...] = mm(pair, scaled, 0, 0).astype(bf16).reshape(send_g.shape)
    exchange(n, me, send_g, grads_ref, sem_g.at[0], sem_g.at[1], "start")
    rows_ref[me] = send_x[me]
    grads_ref[me] = send_g[me]

    heads = ld_ref.shape[1]
    width = u_ref.shape[1]
    log = ld_ref[...]
    upto = jnp.where(t_row >= t_col, 1.0, 0.0)
    run = mm(upto, log, precision=HIGHEST)
    run_t = mm(log, upto, 0, 1, precision=HIGHEST)
    total = run[tok - 1 : tok, :]
    tail_x = spread(jnp.exp(total - run), width)
    tail_ref[...] = tail_x
    ut = (u_ref[...].astype(f32) * tail_x).astype(bf16)
    ut_ref[...] = ut
    st_send[...] = mm(ut, b_ref[...], 0, 0).astype(bf16).reshape(st_send.shape)
    tot_send[...] = jnp.concatenate(
        [
            jnp.broadcast_to(total, (tot_send.shape[0], heads)),
            jnp.zeros((tot_send.shape[0], tot_send.shape[1] - heads), f32),
        ],
        axis=1,
    )

    def totals(act):
        def one(i, _):
            to = lax.rem(me + i, n)
            back = lax.rem(me - i + n, n)
            if act == "start":
                remote(
                    tot_send, tot_ref.at[me], sem_t.at[0, i], sem_t.at[1, i], "ctx", to
                ).start()
            else:
                copy = remote(
                    tot_send, tot_ref.at[back], sem_t.at[0, i], sem_t.at[1, i], "ctx", to
                )
                copy.wait_recv()
                copy.wait_send()
            return 0

        lax.fori_loop(1, n, one, 0)

    totals("start")
    exchange(n, me, st_send, st_recv, sem_s.at[0], sem_s.at[1], "start")
    st_recv[me] = st_send[me]
    tot_ref[me] = tot_send[...]

    er_ref[...] = spread(jnp.exp(run), width)
    affinity = mm(c_ref[...], b_ref[...], 1, 1)
    for h in range(heads):
        gap = run[:, h : h + 1] - run_t[h : h + 1, :]
        decay = jnp.where(t_row >= t_col, jnp.exp(jnp.where(t_row >= t_col, gap, 0.0)), 0.0)
        decay_ref[h] = decay.astype(bf16)
        mix_ref[h] = (decay * affinity).astype(bf16)

    totals("wait")
    exchange(n, me, st_send, st_recv, sem_s.at[0], sem_s.at[1], "wait")
    scan_states(n, me, st_recv, back_send, tot_ref, width // heads, False)
    exchange(n, me, back_send, before_ref, sem_b.at[0], sem_b.at[1], "start")
    before_ref[me] = back_send[me]
    exchange(n, me, send_x, rows_ref, sem_x.at[0], sem_x.at[1], "wait")
    exchange(n, me, send_g, grads_ref, sem_g.at[0], sem_g.at[1], "wait")
    exchange(n, me, back_send, before_ref, sem_b.at[0], sem_b.at[1], "wait")


def dispatch(moe_input, out_grad, ids, prob, counts, ssd_input, in_map, out_map, log_decay):
    n = lax.axis_size("ctx")
    tok, cols = moe_input.shape
    experts = counts.shape[1]
    cap = 2 * tok * ids.shape[1] // experts
    heads = log_decay.shape[1]
    width = ssd_input.shape[1]
    state = in_map.shape[1]
    part = width // n
    block = jax.ShapeDtypeStruct((n, cap, cols), bf16)
    wide = jax.ShapeDtypeStruct((tok, width), f32)
    square = jax.ShapeDtypeStruct((heads, tok, tok), bf16)
    return pl.pallas_call(
        functools.partial(dispatch_kernel, n),
        out_shape=(
            block,
            block,
            jax.ShapeDtypeStruct((tok, experts * cap), bf16),
            wide,
            wide,
            jax.ShapeDtypeStruct((tok, width), bf16),
            square,
            square,
            jax.ShapeDtypeStruct((n, part, state), bf16),
            jax.ShapeDtypeStruct((n, 8, 128), f32),
        ),
        in_specs=[VMEM] * 9,
        out_specs=[VMEM] * 10,
        scratch_shapes=[
            pltpu.VMEM((n, cap, cols), bf16),
            pltpu.VMEM((n, cap, cols), bf16),
            pltpu.VMEM((n, part, state), bf16),
            pltpu.VMEM((n, part, state), bf16),
            pltpu.VMEM((n, part, state), bf16),
            pltpu.VMEM((8, 128), f32),
            DMA((2, n)),
            DMA((2, n)),
            DMA((2, n)),
            DMA((2, n)),
            DMA((2, n)),
        ],
        compiler_params=pltpu.CompilerParams(
            collective_id=0, has_side_effects=True, vmem_limit_bytes=48 * 2**20
        ),
        name="dispatch",
    )(moe_input, out_grad, ids, prob, counts, ssd_input, in_map, out_map, log_decay)


def expert_kernel(
    n,
    n_tp,
    x_ref,
    g_ref,
    pick_ref,
    og_ref,
    wg_hbm,
    wu_hbm,
    wd_hbm,
    out_ref,
    wg,
    wu,
    wd,
    psend,
    precv,
    q,
    ain,
    bin_,
    cin,
    csend,
    gall,
    eg,
    ret,
    wsem,
    psem,
    ringsem,
    gsem,
    rsem,
):
    me = lax.axis_index("ctx")
    t = lax.axis_index("tp")
    ny = n_tp // 2
    y, k = t // 2, lax.rem(t, 2)
    sib = y * 2 + (1 - k)
    y_up, y_dn, y_op = lax.rem(y + 1, ny), lax.rem(y + ny - 1, ny), lax.rem(y + 2, ny)
    up, dn = y_up * 2 + k, y_dn * 2 + k
    loads = [
        pltpu.make_async_copy(src, dst, wsem.at[i])
        for i, (src, dst) in enumerate(((wg_hbm, wg), (wu_hbm, wu), (wd_hbm, wd)))
    ]
    for load in loads:
        load.start()
    hello_ctx(n, me)
    hello_tp((sib, up, dn))

    half = x_ref.shape[0] // 2
    cap = ret.shape[1]
    hidden = wg.shape[1]
    chunk = half // ny
    edge = chunk // 2
    mine, other = k * half, (1 - k) * half

    def product(p, base):
        if p == 0:
            return mm(x_ref[pl.ds(base, half), :], wg[...]).astype(bf16)
        if p == 1:
            return mm(x_ref[pl.ds(base, half), :], wu[...]).astype(bf16)
        return mm(g_ref[pl.ds(base, half), :], wd[...], 1, 1).astype(bf16)

    pair = []
    for p in range(3):
        loads[p].wait()
        psend[p] = product(p, other)
        if p == 0:
            pl.semaphore_wait(pltpu.get_barrier_semaphore(), n - 1 + 3)
        copy = remote(psend.at[p], precv.at[p], psem.at[0, p], psem.at[1, p], "tp", sib)
        copy.start()
        pair.append(copy)
    for p in range(3):
        q[p] = product(p, mine)
    for p in range(3):
        pair[p].wait_recv()

    def rows(place, lo, size):
        return pl.ds(pl.multiple_of(place * chunk + lo, 16), size)

    def join(place):
        at = rows(place, 0, chunk)
        q[:, at, :] = (q[:, at, :].astype(f32) + precv[:, at, :].astype(f32)).astype(bf16)

    def ring(i, src, dst, place):
        copy = remote(src, dst, ringsem.at[0, i], ringsem.at[1, i], "tp", place)
        copy.start()
        return copy

    join(y_op)
    a_up = ring(0, q.at[:, rows(y_op, 0, edge), :], ain.at[0], up)
    a_dn = ring(1, q.at[:, rows(y_op, edge, edge), :], ain.at[1], dn)
    join(y_up)
    b_up = ring(2, q.at[:, rows(y_up, edge, edge), :], bin_.at[0], up)
    join(y_dn)
    b_dn = ring(3, q.at[:, rows(y_dn, 0, edge), :], bin_.at[1], dn)
    join(y)
    a_up.wait_recv()
    csend[0] = (q[:, rows(y_up, 0, edge), :].astype(f32) + ain[0].astype(f32)).astype(bf16)
    c_up = ring(4, csend.at[0], cin.at[0], up)
    a_dn.wait_recv()
    csend[1] = (q[:, rows(y_dn, edge, edge), :].astype(f32) + ain[1].astype(f32)).astype(bf16)
    c_dn = ring(5, csend.at[1], cin.at[1], dn)
    b_up.wait_recv()
    b_dn.wait_recv()
    c_up.wait_recv()
    c_dn.wait_recv()

    start = mine + y * chunk
    for e in range(2):
        total = (
            q[:, rows(y, e * edge, edge), :].astype(f32)
            + cin[e].astype(f32)
            + bin_[1 - e].astype(f32)
        )
        gate, upv, back = total[0], total[1], total[2]
        sigma = 1.0 / (1.0 + jnp.exp(-gate))
        at = pl.ds(pl.multiple_of(start + e * edge, 16), edge)
        gall[at, 0:hidden] = (back * upv * sigma * (1.0 + gate * (1.0 - sigma))).astype(bf16)
        gall[at, hidden : 2 * hidden] = (back * gate * sigma).astype(bf16)

    def share(i, base, place, lo, size, to):
        at = gall.at[pl.ds(pl.multiple_of(base + place * chunk + lo, 16), size), :]
        copy = remote(at, at, gsem.at[0, i], gsem.at[1, i], "tp", to)
        copy.start()
        return copy

    def arrived(i, base, place, lo, size):
        at = gall.at[pl.ds(pl.multiple_of(base + place * chunk + lo, 16), size), :]
        remote(at, at, gsem.at[0, i], gsem.at[1, i], "tp", sib).wait_recv()

    sent = [
        share(0, mine, y, 0, chunk, up),
        share(1, mine, y, 0, chunk, dn),
        share(2, mine, y, 0, chunk, sib),
    ]
    arrived(0, mine, y_dn, 0, chunk)
    sent.append(share(3, mine, y_dn, 0, edge, up))
    sent.append(share(5, mine, y_dn, 0, chunk, sib))
    arrived(1, mine, y_up, 0, chunk)
    sent.append(share(4, mine, y_up, edge, edge, dn))
    sent.append(share(6, mine, y_up, 0, chunk, sib))
    arrived(3, mine, y_op, 0, edge)
    arrived(4, mine, y_op, edge, edge)
    sent.append(share(7, mine, y_op, 0, chunk, sib))

    def back_product(base):
        at = pl.ds(pl.multiple_of(base, 16), half)
        grad = mm(gall[at, 0:hidden], wg[...], 1, 1) + mm(
            gall[at, hidden : 2 * hidden], wu[...], 1, 1
        )
        return grad.astype(bf16).reshape(n // 2, cap, grad.shape[1])

    def give(first):
        def one(i, _):
            to = first + lax.rem(me + i, n // 2)

            @pl.when(to != me)
            def _():
                remote(eg.at[to], ret.at[me], rsem.at[0, to], rsem.at[1, me], "ctx", to).start()

            return 0

        lax.fori_loop(0, n // 2, one, 0)

    first, second = k * (n // 2), (1 - k) * (n // 2)
    eg[pl.ds(first, n // 2)] = back_product(mine)
    give(first)
    arrived(2, other, y, 0, chunk)
    arrived(5, other, y_dn, 0, chunk)
    arrived(6, other, y_up, 0, chunk)
    arrived(7, other, y_op, 0, chunk)
    eg[pl.ds(second, n // 2)] = back_product(other)
    give(second)
    ret[me] = eg[me]

    for copy in pair + [a_up, a_dn, b_up, b_dn, c_up, c_dn] + sent:
        copy.wait_send()

    def finish(i, _):
        it = lax.rem(me + i, n)
        copy = remote(eg.at[it], ret.at[it], rsem.at[0, it], rsem.at[1, it], "ctx", it)
        copy.wait_send()
        copy.wait_recv()
        return 0

    lax.fori_loop(1, n, finish, 0)
    entries = ret[...].reshape(n * cap, ret.shape[2])
    out_ref[...] = (og_ref[...].astype(f32) + mm(pick_ref[...], entries)).astype(bf16)


def experts(rows, grads, pick, out_grad, w_gate, w_up, w_down):
    n = lax.axis_size("ctx")
    n_tp = lax.axis_size("tp")
    _, cap, cols = rows.shape
    hidden = w_gate.shape[1]
    total = n * cap
    half = total // 2
    edge = half // (n_tp // 2) // 2
    flat = (total, cols)
    return pl.pallas_call(
        functools.partial(expert_kernel, n, n_tp),
        out_shape=jax.ShapeDtypeStruct(out_grad.shape, bf16),
        in_specs=[VMEM] * 4 + [ANY] * 3,
        out_specs=VMEM,
        scratch_shapes=[
            pltpu.VMEM(w_gate.shape, bf16),
            pltpu.VMEM(w_up.shape, bf16),
            pltpu.VMEM(w_down.shape, bf16),
            pltpu.VMEM((3, half, hidden), bf16),
            pltpu.VMEM((3, half, hidden), bf16),
            pltpu.VMEM((3, half, hidden), bf16),
            pltpu.VMEM((2, 3, edge, hidden), bf16),
            pltpu.VMEM((2, 3, edge, hidden), bf16),
            pltpu.VMEM((2, 3, edge, hidden), bf16),
            pltpu.VMEM((2, 3, edge, hidden), bf16),
            pltpu.VMEM((total, 2 * hidden), bf16),
            pltpu.VMEM((n, cap, cols), bf16),
            pltpu.VMEM((n, cap, cols), bf16),
            DMA((3,)),
            DMA((2, 3)),
            DMA((2, 6)),
            DMA((2, 8)),
            DMA((2, n)),
        ],
        compiler_params=pltpu.CompilerParams(
            collective_id=1, has_side_effects=True, vmem_limit_bytes=56 * 2**20
        ),
        name="experts",
    )(rows.reshape(flat), grads.reshape(flat), pick, out_grad, w_gate, w_up, w_down)


def head_kernel(
    n,
    n_tp,
    ig_ref,
    u_ref,
    b_ref,
    c_ref,
    er_ref,
    tail_ref,
    ut_ref,
    decay_ref,
    mix_ref,
    before_ref,
    tot_ref,
    w_hbm,
    scan_ref,
    in_ref,
    out_ref,
    w,
    gat,
    acc,
    intra,
    st_send,
    st_recv,
    back_send,
    after,
    wsem,
    gsem,
    sem_s,
    sem_b,
):
    me = lax.axis_index("ctx")
    t = lax.axis_index("tp")
    ny = n_tp // 2
    y, k = t // 2, lax.rem(t, 2)
    sib = y * 2 + (1 - k)
    y_up, y_dn, y_op = lax.rem(y + 1, ny), lax.rem(y + ny - 1, ny), lax.rem(y + 2, ny)
    up, dn = y_up * 2 + k, y_dn * 2 + k
    op = y_op * 2 + k
    tok, cols = ig_ref.shape
    loads = []
    for part in range(n_tp):
        load = pltpu.make_async_copy(
            w_hbm.at[pl.ds(part * cols, cols), :], w.at[part], wsem.at[part]
        )
        load.start()
        loads.append(load)
    hello_ctx(n, me)
    hello_tp((sib, up, dn))
    gat[t] = ig_ref[...]
    pl.semaphore_wait(pltpu.get_barrier_semaphore(), n - 1 + 3)

    def share(i, place, lo, size, to):
        at = gat.at[place, pl.ds(lo, size), :]
        copy = remote(at, at, gsem.at[0, i], gsem.at[1, i], "tp", to)
        copy.start()
        return copy

    def arrived(i, place, lo, size):
        at = gat.at[place, pl.ds(lo, size), :]
        remote(at, at, gsem.at[0, i], gsem.at[1, i], "tp", sib).wait_recv()

    edge = tok // 2
    sent = [share(0, t, 0, tok, up), share(1, t, 0, tok, dn), share(2, t, 0, tok, sib)]
    for load in loads:
        load.wait()

    def add(place):
        acc[...] += mm(gat[place], w[place])

    acc[...] = mm(gat[t], w[t])
    arrived(2, sib, 0, tok)
    add(sib)
    arrived(0, dn, 0, tok)
    sent.append(share(3, dn, 0, edge, up))
    sent.append(share(5, dn, 0, tok, sib))
    arrived(1, up, 0, tok)
    sent.append(share(4, up, edge, edge, dn))
    sent.append(share(6, up, 0, tok, sib))
    add(dn)
    add(up)
    arrived(3, op, 0, edge)
    arrived(4, op, edge, edge)
    sent.append(share(7, op, 0, tok, sib))
    add(op)
    sdn, sup, sop = y_dn * 2 + (1 - k), y_up * 2 + (1 - k), y_op * 2 + (1 - k)
    arrived(5, sdn, 0, tok)
    add(sdn)
    arrived(6, sup, 0, tok)
    add(sup)
    arrived(7, sop, 0, tok)
    add(sop)

    grad = acc[...].astype(bf16)
    ge = (grad.astype(f32) * er_ref[...]).astype(bf16)
    st_send[...] = mm(ge, c_ref[...], 0, 0).astype(bf16).reshape(st_send.shape)
    exchange(n, me, st_send, st_recv, sem_s.at[0], sem_s.at[1], "start")
    st_recv[me] = st_send[me]

    heads = decay_ref.shape[0]
    size = grad.shape[1] // heads
    weights = jnp.zeros((tok, tok), f32)
    for h in range(heads):
        gh = grad[:, h * size : (h + 1) * size]
        uh = u_ref[:, h * size : (h + 1) * size]
        weights = weights + decay_ref[h].astype(f32) * mm(gh, uh, 1, 1)
        intra[:, h * size : (h + 1) * size] = mm(mix_ref[h], gh, 0, 0)
    weights = weights.astype(bf16)
    state = b_ref.shape[1]
    out_ref[...] = mm(weights, b_ref[...]) + mm(ge, before_ref[...].reshape(-1, state))

    exchange(n, me, st_send, st_recv, sem_s.at[0], sem_s.at[1], "wait")
    scan_states(n, me, st_recv, back_send, tot_ref, size, True)
    exchange(n, me, back_send, after, sem_b.at[0], sem_b.at[1], "start")
    after[me] = back_send[me]
    in_part = mm(weights, c_ref[...], 0, 0)
    for copy in sent:
        copy.wait_send()
    exchange(n, me, back_send, after, sem_b.at[0], sem_b.at[1], "wait")
    later = after[...].reshape(-1, state)
    in_ref[...] = in_part + mm(ut_ref[...], later)
    scan_ref[...] = (intra[...] + tail_ref[...] * mm(b_ref[...], later, 1, 1)).astype(bf16)


def head_part(input_grad, ssd_input, in_map, out_map, prepared, weight):
    n = lax.axis_size("ctx")
    n_tp = lax.axis_size("tp")
    tok, cols = input_grad.shape
    width = ssd_input.shape[1]
    state = in_map.shape[1]
    part = width // n
    small = jax.ShapeDtypeStruct((tok, state), f32)
    return pl.pallas_call(
        functools.partial(head_kernel, n, n_tp),
        out_shape=(jax.ShapeDtypeStruct((tok, width), bf16), small, small),
        in_specs=[VMEM] * 11 + [ANY],
        out_specs=[VMEM] * 3,
        scratch_shapes=[
            pltpu.VMEM((n_tp, cols, width), bf16),
            pltpu.VMEM((n_tp, tok, cols), bf16),
            pltpu.VMEM((tok, width), f32),
            pltpu.VMEM((tok, width), f32),
            pltpu.VMEM((n, part, state), bf16),
            pltpu.VMEM((n, part, state), bf16),
            pltpu.VMEM((n, part, state), bf16),
            pltpu.VMEM((n, part, state), bf16),
            DMA((n_tp,)),
            DMA((2, 8)),
            DMA((2, n)),
            DMA((2, n)),
        ],
        compiler_params=pltpu.CompilerParams(
            collective_id=2, has_side_effects=True, vmem_limit_bytes=48 * 2**20
        ),
        name="heads",
    )(input_grad, ssd_input, in_map, out_map, *prepared, weight)


def body(
    moe_input,
    out_grad,
    route_prob,
    route_ids,
    route_counts,
    w_gate,
    w_up,
    w_down,
    out_weight,
    ssd_input,
    input_map,
    output_map,
    log_decay,
):
    weight = lax.all_gather(out_weight, "ctx", axis=0, tiled=True)
    rows, grads, pick, *prepared = dispatch(
        moe_input,
        out_grad,
        route_ids,
        route_prob,
        route_counts,
        ssd_input,
        input_map,
        output_map,
        log_decay,
    )
    input_grad = experts(rows, grads, pick, out_grad, w_gate[0], w_up[0], w_down[0])
    scan_grad, in_map_grad, out_map_grad = head_part(
        input_grad, ssd_input, input_map, output_map, prepared, weight
    )
    return (input_grad, scan_grad, in_map_grad, out_map_grad)


def solution(mesh):
    in_specs = (
        P("ctx", "tp"),
        P("ctx", "tp"),
        P("ctx", None),
        P("ctx", None),
        P("ctx", None),
        P("ctx", "tp", None),
        P("ctx", "tp", None),
        P("ctx", None, "tp"),
        P("ctx", "tp"),
        P("ctx", "tp"),
        P("ctx", "tp"),
        P("ctx", "tp"),
        P("ctx", "tp"),
    )
    out_specs = (P("ctx", "tp"), P("ctx", "tp"), P("ctx", "tp"), P("ctx", "tp"))
    return jax.shard_map(body, mesh=mesh, in_specs=in_specs, out_specs=out_specs, check_vma=False)
```

time: 627 us -> 240 us (0.38)
  waiting for transfers between devices: 426 us -> 0.68 us
  Pallas kernels: 0 us -> 206 us
  other arithmetic: 63.1 us -> 0 us
  matrix products: 37.2 us -> 0 us
  blocking collectives: 32.3 us -> 0 us
  starting transfers between devices: 30.7 us -> 0.04 us
    all_gather x4 -> x1, waiting for transfers between devices: 298 us -> 0.01 us  [body(): weight = lax.all_gather(out_weight, 'ctx', axis=0, tiled=True)]
    pallas_call x0 -> x3, Pallas kernels: none -> 206 us  [the longest x1 87.4 us: dispatch(): pl.pallas_call(functools.partial(dispatch_kernel, n), out_shape=(block, b...]
    psum x1 -> x0, waiting for transfers between devices: 79.2 us -> none  [body(): lax.psum(gate_part.astype(jnp.bfloat16), 'tp').astype(jnp.float32)]
    all_to_all x3 -> x0, waiting for transfers between devices: 47.1 us -> none  [the longest x1 19.4 us: body(): lax.all_to_all(returned, 'ctx', split_axis=0, concat_axis=0, tiled=True)]
    dot_general x16 -> x0, matrix products: 37.2 us -> none  [the longest x1 7.12 us: body(): jnp.dot(full_grad, lax.all_gather(out_weight, 'ctx', axis=0, tiled=True),...]
    add x31 -> x0, other arithmetic: 34.2 us -> none  [chain_combine(): later[1] + later[0][:, None, None] * earlier[1]]
    all_gather x1 -> x0, blocking collectives: 32.3 us -> none  [entering(): lax.all_gather(a.astype(kind), axis)]
    all_to_all x3 -> x0, starting transfers between devices: 30.1 us -> none  [the longest x1 12.1 us: body(): lax.all_to_all(send_rows, 'ctx', split_axis=0, concat_axis=0, tiled=True)]
  transfers between devices with their start and end apart: 8 -> 1, of which waited for: 8 -> 0; matrix products, arithmetic and copies ran while one was open for 5% -> 5% of each run, Pallas kernels for 0% -> 70%
where the time goes in v1:
time: 240 us
  Pallas kernels  206 us (86%)
  local copies, waits for them, and re-layouts  18.5 us (8%)
  between operations  14.1 us (6%)
    pallas_call x1, Pallas kernels, dispatch(): pl.pallas_call(functools.partial(dispatch_kernel, n), out_shape=(block, b...  87.4 us
    pallas_call x1, Pallas kernels, experts(): pl.pallas_call(functools.partial(expert_kernel, n, n_tp), out_shape=jax.S...  80.1 us
    pallas_call x1, Pallas kernels, head_part(): pl.pallas_call(functools.partial(head_kernel, n, n_tp), out_shape=(jax.Sh...  39 us
    unnamed x36, local copies, waits for them, and re-layouts  18.5 us
  transfers between devices with their start and end apart: 1, of which 0 were waited for; matrix products, arithmetic and copies ran while one was open for 5% of the time, Pallas kernels for 70%

profile of v1, /device:TPU:1, one launch (start us, length us, event | category | flops | bytes accessed | tf_op | source)
XLA Modules:
  0.0 239.8 jit_solution(13722423571353644867)
XLA Ops:
  7.2 0.0 all-gather.2.cloned.1.call-start
  7.2 0.7 all-gather.2.cloned.1.call-update
  7.9 1.1 copy.18.g_ref.og_ref
  9.0 0.0 copy-start.1
  9.0 1.2 copy.17.x_ref
  10.2 0.8 copy.19.ids_ref
  11.0 0.8 copy.20.prob_ref
  11.7 0.8 copy.21.ld_ref
  12.5 0.0 copy-start.12
  12.6 4.5 %copy.22 = bf16[1,1536,800]{2,1,0:T(8,128)(2,1)} copy(bf16[1,1536,800]{1,2,0:T(8,128)(2,1)} %param.20) | data formatting | bytes 4915200 | tf_op args[7]
  17.1 0.0 copy-done.1
  17.1 0.0 copy-done.2
  17.1 0.0 copy-done.12
  17.1 0.0 copy-start.8
  17.1 0.7 copy-done.8
  17.8 0.8 copy-done.10
  18.6 87.4 %dispatch.1 = (bf16[32,16,800]{2,1,0:T(8,128)(2,1)S(1)}, bf16[32,16,800]{2,1,0:T(8,128)(2,1)S(1)}, bf16[128,512]{1,0:T(8,128)(2,1)S(1)}, f32[128,1024]{1,0:T(8,1...) custom-call(bf16[128,800]{1,0:T(8,128)(2,1)S(1)} %copy.17.x_ref, ...), custom_call_target="tpu_custom_call" | custom-call | tf_op jit(solution)/shard_map/dispatch/pallas_call | solution.py:232
  106.0 0.0 copy-start.3
  106.0 0.9 copy-done.3
  107.0 0.9 copy-done.4
  107.9 0.7 copy-done.5
  108.5 0.7 copy-done.7
  109.2 80.1 %experts.1.ig_ref = bf16[128,800]{1,0:T(8,128)(2,1)} custom-call(bf16[512,800]{1,0:T(8,128)(2,1)} %bitcast.5, bf16[512,800]{1,0:T(8,128)(2,1)} %bitcast.6, bf16[128,512]{1,0:T(8,128)(2,1)} %copy-done.7, bf16[128,800]{1,0:T(8,128)(2,1)} %copy-done.1, bf16[800,1536]{1,0:T(8,128)(2,1)} %bitcast.8, bf16[800,1536]{1,0:T(8,128)(2,1)} %bitcast.9, ...), custom_call_target="tpu_custom_call" | custom-call | tf_op jit(solution)/shard_map/experts/pallas_call | solution.py:465
  189.3 1.8 copy.24
  191.0 0.0 copy-done.6
  191.0 0.0 copy-done.9
  191.0 0.0 copy-done.11
  191.1 0.9 copy-done
  192.0 39.0 %heads.1 = (bf16[128,1024]{1,0:T(8,128)(2,1)S(1)}, f32[128,128]{1,0:T(8,128)S(1)}, f32[128,128]{1,0:T(8,128)S(1)}) custom-call(bf16[128,800]{1,0:T(8,128)(2,1)S(1)} %copy-done, bf16[128,1024]{1,0:T(8,128)(2,1)S(1)} %copy-done.2, bf16[128,128]{1,0:T(8,128)(2,1)S(1)} %copy-done.9, bf16[128,128]{1,0:T(8,128)(2,1)S(1)} %copy-done.11, ...), custom_call_target="tpu_custom_call" | custom-call | tf_op jit(solution)/shard_map/heads/pallas_call | solution.py:629
  231.0 0.7 copy.28
  231.7 0.6 copy.29
  232.3 0.6 copy.30
  (10 shorter events, 0.0 us)
Async XLA Ops:
  7.2 183.9 %all-gather.2.cloned.1.call-start = ((), (), s32[]{:S(2)}) async-start(), calls=%async_computation | async-start | bytes 13516800 | tf_op jit(solution)/shard_map/all_gather | solution.py:670
  9.0 8.1 %copy-start.1 = (bf16[128,800]{1,0:T(8,128)(2,1)}, bf16[128,800]{1,0:T(8,128)(2,1)S(1)}, u32[]{:S(2)}) copy-start(bf16[128,800]{1,0:T(8,128)(2,1)S(1)} %copy.18.g_ref.og_ref) | copy-start | bytes 614404
  12.5 4.5 %copy-start.2 = (bf16[128,1024]{1,0:T(8,128)(2,1)S(1)}, bf16[128,1024]{1,0:T(8,128)(2,1)}, u32[]{:S(2)}) copy-start(bf16[128,1024]{1,0:T(8,128)(2,1)} %u_ref.3) | copy-start | bytes 786436
  12.5 4.5 %copy-start.12 = (s32[1,32]{1,0:T(1,128)S(1)}, s32[1,32]{1,0:T(1,128)}, u32[]{:S(2)}) copy-start(s32[1,32]{1,0:T(1,128)} %counts_ref.1) | copy-start | bytes 388
  17.1 0.8 copy-start.8
  17.8 0.8 copy-start.10
  106.0 1.0 copy-start.3
  107.0 0.9 copy-start.4
  107.9 0.7 copy-start.5
  108.5 0.7 copy-start.7
  109.2 81.9 %copy-start.6 = (f32[32,8,128]{2,1,0:T(8,128)S(1)}, f32[32,8,128]{2,1,0:T(8,128)}, u32[]{:S(2)}) copy-start(f32[32,8,128]{2,1,0:T(8,128)} %copy-done.5) | copy-start | bytes 393220
  109.2 81.9 %copy-start.9 = (bf16[128,128]{1,0:T(8,128)(2,1)S(1)}, bf16[128,128]{1,0:T(8,128)(2,1)}, u32[]{:S(2)}) copy-start(bf16[128,128]{1,0:T(8,128)(2,1)} %b_ref.3) | copy-start | bytes 98308
  109.2 81.9 %copy-start.11 = (bf16[128,128]{1,0:T(8,128)(2,1)S(1)}, bf16[128,128]{1,0:T(8,128)(2,1)}, u32[]{:S(2)}) copy-start(bf16[128,128]{1,0:T(8,128)(2,1)} %c_ref.3) | copy-start | bytes 98308
  191.0 0.9 copy-start
Sparse Core Ops, SparseCore 0:
  10.6 162.6 all-gather.1

commit v2 on v0

v2 whole, which is shorter than its diff:
```python
import functools

import jax
import jax.numpy as jnp
from jax import lax
from jax.experimental import pallas as pl
from jax.experimental.pallas import tpu as pltpu
from jax.sharding import PartitionSpec as P

MESH = pl.DeviceIdType.MESH
HIGHEST = lax.Precision.HIGHEST
bf16, f32, i32 = jnp.bfloat16, jnp.float32, jnp.int32
VMEM = pl.BlockSpec(memory_space=pltpu.VMEM)
ANY = pl.BlockSpec(memory_space=pl.ANY)
DMA = pltpu.SemaphoreType.DMA


def mm(a, b, ca=1, cb=0, precision=None):
    return lax.dot_general(
        a, b, (((ca,), (cb,)), ((), ())), precision=precision, preferred_element_type=f32
    )


def remote(src, dst, send, recv, axis, place):
    return pltpu.make_async_remote_copy(
        src_ref=src,
        dst_ref=dst,
        send_sem=send,
        recv_sem=recv,
        device_id={axis: place},
        device_id_type=MESH,
    )


def hello_ctx(n, me):
    barrier = pltpu.get_barrier_semaphore()

    def one(i, _):
        pl.semaphore_signal(
            barrier, inc=1, device_id={"ctx": lax.rem(me + i, n)}, device_id_type=MESH
        )
        return 0

    lax.fori_loop(1, n, one, 0)


def hello_tp(places):
    barrier = pltpu.get_barrier_semaphore()
    for place in places:
        pl.semaphore_signal(barrier, inc=1, device_id={"tp": place}, device_id_type=MESH)


def exchange(n, me, src, dst, send, recv, act):
    def one(i, _):
        to = lax.rem(me + i, n)
        back = lax.rem(me - i + n, n)
        if act == "start":
            remote(src.at[to], dst.at[me], send.at[i], recv.at[i], "ctx", to).start()
        else:
            copy = remote(src.at[to], dst.at[back], send.at[i], recv.at[i], "ctx", to)
            copy.wait_recv()
            copy.wait_send()
        return 0

    lax.fori_loop(1, n, one, 0)


def spread(columns, total):
    heads = columns.shape[1]
    size = total // heads
    put = lax.broadcasted_iota(i32, (heads, total), 1) // size == lax.broadcasted_iota(
        i32, (heads, total), 0
    )
    return mm(columns, put.astype(f32), precision=HIGHEST)


def scan_states(n, me, loc, out, totals, rows_per_head, backward):
    head = me * loc.shape[1] // rows_per_head
    lane = lax.broadcasted_iota(i32, totals.shape, 2)
    decay = jnp.exp(jnp.sum(jnp.where(lane == head, totals[...], 0.0), axis=2, keepdims=True))
    state = jnp.zeros(loc.shape[1:], f32)
    order = range(n - 1, -1, -1) if backward else range(n)
    for c in order:
        out[c] = state.astype(bf16)
        state = decay[c, 0:1, :] * state + loc[c].astype(f32)


def layer_kernel(
    nx,
    nz,
    ny,
    x_ref,
    g_ref,
    ids_ref,
    prob_ref,
    counts_ref,
    u_ref,
    b_ref,
    c_ref,
    ld_ref,
    wg_hbm,
    wu_hbm,
    wd_hbm,
    w_hbm,
    out_ref,
    scan_ref,
    in_ref,
    out_map_ref,
    er_ref,
    tail_ref,
    ut_ref,
    decay_ref,
    mix_ref,
    before_ref,
    tot_ref,
    wg,
    wu,
    wd,
    send,
    inbuf,
    part,
    precv,
    rsum,
    gall,
    eg,
    ret,
    pick,
    st_send,
    st_recv,
    back_send,
    tot_send,
    w,
    ya,
    xa,
    hsend,
    hrecv,
    intra,
    gst_send,
    gst_recv,
    gback_send,
    after,
    wsem,
    isem,
    psem,
    ssem,
    gsem,
    fsem,
    rsem,
    sem_s,
    sem_t,
    sem_b,
    usem,
    dsem,
    ysem,
    xsem,
    hfsem,
    hsem,
    gsem_s,
    gsem_b,
):
    n = nx * nz
    me = lax.axis_index("ctx")
    x, z = me // nz, lax.rem(me, nz)
    t = lax.axis_index("tp")
    y, k = t // 2, lax.rem(t, 2)
    sib = y * 2 + (1 - k)
    y_up, y_dn, y_op = lax.rem(y + 1, ny), lax.rem(y + ny - 1, ny), lax.rem(y + 2, ny)
    up, dn, op = y_up * 2 + k, y_dn * 2 + k, y_op * 2 + k

    def ahead(dx, dz):
        return lax.rem(x + dx, nx) * nz + lax.rem(z + dz, nz)

    def behind(dx, dz):
        return lax.rem(x - dx + nx, nx) * nz + lax.rem(z - dz + nz, nz)

    cols, tok = x_ref.shape
    hidden = wg.shape[1]
    cut = wd_hbm.shape[0] // 128 * 128
    loads = [
        pltpu.make_async_copy(wg_hbm, wg.at[pl.ds(0, cols)], wsem.at[0]),
        pltpu.make_async_copy(wu_hbm, wu.at[pl.ds(0, cols)], wsem.at[1]),
        pltpu.make_async_copy(wd_hbm.at[pl.ds(0, cut)], wd.at[pl.ds(0, cut)], wsem.at[2]),
        pltpu.make_async_copy(
            wd_hbm.at[pl.ds(cut, cols - cut)], wd.at[pl.ds(cols, cols - cut)], wsem.at[3]
        ),
    ]
    own_w = pltpu.make_async_copy(w_hbm, w.at[z], wsem.at[4])
    own_w.start()
    for load in loads:
        load.start()
    hello_ctx(n, me)
    hello_tp((sib, up, dn, op))

    experts = counts_ref.shape[1]
    cap = inbuf.shape[2]
    slots = experts * cap
    rest = cols - cut
    full = cut + 128
    ids = ids_ref[...]
    names = lax.broadcasted_iota(i32, (experts, tok), 0)
    m0 = ids[0:1, :] == names
    m1 = ids[1:2, :] == names
    member = jnp.where(m0, 1.0, 0.0) + jnp.where(m1, 1.0, 0.0)
    t_row = lax.broadcasted_iota(i32, (tok, tok), 0)
    t_col = lax.broadcasted_iota(i32, (tok, tok), 1)
    rank = mm(member.astype(bf16), jnp.where(t_row < t_col, 1.0, 0.0).astype(bf16))
    e_row = lax.broadcasted_iota(i32, (experts, experts), 0)
    e_col = lax.broadcasted_iota(i32, (experts, experts), 1)
    limit = jnp.sum(
        jnp.where(e_row == e_col, counts_ref[...].astype(f32), 0.0), axis=1, keepdims=True
    )
    slot = jnp.where(rank < limit, rank + (names * cap).astype(f32), -1.0)
    place = lax.broadcasted_iota(i32, (slots, tok), 0).astype(f32)
    p0 = jnp.where(place == jnp.sum(jnp.where(m0, slot, 0.0), 0, keepdims=True), 1.0, 0.0)
    p1 = jnp.where(place == jnp.sum(jnp.where(m1, slot, 0.0), 0, keepdims=True), 1.0, 0.0)
    both = (p0 + p1).astype(bf16)
    pick[...] = both

    pl.semaphore_wait(pltpu.get_barrier_semaphore(), n - 1 + 4)
    mid = w.shape[2] // 2
    last_hop = nz // 2 - 1

    def w_copy(j, upward):
        if upward:
            block, to, sem = lax.rem(z - j + nz, nz), ahead(0, 1), usem
        else:
            block, to, sem = lax.rem(z + j, nz), behind(0, 1), dsem
        if j < last_hop:
            at = w.at[block]
        else:
            at = w.at[block, :, pl.ds(0 if upward else mid, mid)]
        return remote(at, at, sem.at[0, j], sem.at[1, j], "ctx", to)

    def w_landed(j):
        for upward, sem in ((True, usem), (False, dsem)):
            block = lax.rem(z - j - 1 + nz, nz) if upward else lax.rem(z + j + 1, nz)
            if j < last_hop:
                at = w.at[block]
            else:
                at = w.at[block, :, pl.ds(0 if upward else mid, mid)]
            remote(at, at, sem.at[0, j], sem.at[1, j], "ctx", ahead(0, 1)).wait_recv()

    def w_hop(j):
        if j:
            w_landed(j - 1)
        w_copy(j, True).start()
        w_copy(j, False).start()

    own_w.wait()
    w_hop(0)
    grad = g_ref[...].astype(f32)
    prob = prob_ref[...]
    scaled = jnp.concatenate(
        [(prob[0:1, :] * grad).astype(bf16), (prob[1:2, :] * grad).astype(bf16)], axis=1
    )
    pair = jnp.concatenate([p0.astype(bf16), p1.astype(bf16)], axis=1)
    sel_x = mm(both, x_ref[...], 1, 1)
    sel_g = mm(pair, scaled, 1, 1)
    send[:, :, 0:cut] = sel_x[:, 0:cut].astype(bf16).reshape(experts, cap, cut)
    send[:, :, cut : 2 * cut] = sel_g[:, 0:cut].astype(bf16).reshape(experts, cap, cut)
    last = jnp.concatenate(
        [sel_x[:, cut:], sel_g[:, cut:], jnp.zeros((slots, 128 - 2 * rest), f32)], axis=1
    )
    send[:, :, 2 * cut :] = last.astype(bf16).reshape(experts, cap, 128)

    def post(i, _):
        dx, dz = i // nz, lax.rem(i, nz)
        to = ahead(dx, dz)
        remote(
            send.at[to], inbuf.at[dx, dz], isem.at[0, i], isem.at[1, i], "ctx", to
        ).start()
        return 0

    lax.fori_loop(1, 2 * nz, post, 0)
    inbuf[0, 0] = send[me]

    heads = ld_ref.shape[0]
    width = u_ref.shape[1]
    log = ld_ref[...]
    upto = jnp.where(t_row >= t_col, 1.0, 0.0)
    run = mm(upto, log, 1, 1, precision=HIGHEST)
    run_t = mm(log, upto, 1, 1, precision=HIGHEST)
    total = run[tok - 1 : tok, :]
    tail_x = spread(jnp.exp(total - run), width)
    tail_ref[...] = tail_x
    ut = (u_ref[...].astype(f32) * tail_x).astype(bf16)
    ut_ref[...] = ut
    st_send[...] = mm(ut, b_ref[...], 0, 0).astype(bf16).reshape(st_send.shape)
    tot_send[...] = jnp.concatenate(
        [
            jnp.broadcast_to(total, (tot_send.shape[0], heads)),
            jnp.zeros((tot_send.shape[0], tot_send.shape[1] - heads), f32),
        ],
        axis=1,
    )

    def totals(act):
        def one(i, _):
            to = lax.rem(me + i, n)
            back = lax.rem(me - i + n, n)
            if act == "start":
                remote(
                    tot_send, tot_ref.at[me], sem_t.at[0, i], sem_t.at[1, i], "ctx", to
                ).start()
            else:
                copy = remote(
                    tot_send, tot_ref.at[back], sem_t.at[0, i], sem_t.at[1, i], "ctx", to
                )
                copy.wait_recv()
                copy.wait_send()
            return 0

        lax.fori_loop(1, n, one, 0)


    wg[pl.ds(cols, 128 - rest), :] = jnp.zeros((128 - rest, hidden), bf16)
    wu[pl.ds(cols, 128 - rest), :] = jnp.zeros((128 - rest, hidden), bf16)
    wd[pl.ds(cut, rest), :] = jnp.zeros((rest, hidden), bf16)
    wd[pl.ds(cols + rest, 128 - 2 * rest), :] = jnp.zeros((128 - 2 * rest, hidden), bf16)
    for load in loads:
        load.wait()

    er_ref[...] = spread(jnp.exp(run), width)
    affinity = mm(c_ref[...], b_ref[...], 1, 1)
    for h in range(heads):
        gap = run[:, h : h + 1] - run_t[h : h + 1, :]
        decay = jnp.where(t_row >= t_col, jnp.exp(jnp.where(t_row >= t_col, gap, 0.0)), 0.0)
        decay_ref[h] = decay.astype(bf16)
        mix_ref[h] = (decay * affinity).astype(bf16)

    half = nz // 2 * cap
    mine, other = pl.multiple_of(k * half, cap), pl.multiple_of((1 - k) * half, cap)

    def pair_copy(s, p):
        return remote(
            part.at[s, p, pl.ds(other, half)],
            precv.at[s, p],
            psem.at[0, s, p],
            psem.at[1, s, p],
            "tp",
            sib,
        )

    def sum_copy(s, i):
        to, dz = ((up, y_up), (dn, y_dn), (op, y_op))[i]
        return remote(
            part.at[s, :, pl.ds(pl.multiple_of(mine + dz * cap, cap), cap)],
            rsum.at[s, i],
            ssem.at[0, s, i],
            ssem.at[1, s, i],
            "tp",
            to,
        )

    def grads_at(s, core, dz):
        return gall.at[s, pl.ds(pl.multiple_of(core * half + dz * cap, cap), cap)]

    froms = (y_dn, y_up, y_op)

    def grad_copy(s, i, dz):
        at = grads_at(s, k, dz)
        return remote(at, at, gsem.at[0, s, i], gsem.at[1, s, i], "tp", (up, dn, op)[i])

    def fwd_copy(s, i, core, dz):
        at = grads_at(s, core, dz)
        return remote(at, at, fsem.at[0, s, i], fsem.at[1, s, i], "tp", sib)

    def first(s):
        def one(i, _):
            @pl.when(s * nz + i > 0)
            def _():
                remote(
                    send.at[ahead(s, i)],
                    inbuf.at[s, i],
                    isem.at[0, s * nz + i],
                    isem.at[1, s * nz + i],
                    "ctx",
                    ahead(s, i),
                ).wait_recv()

            return 0

        lax.fori_loop(0, nz, one, 0)
        rows = inbuf[s].reshape(nz * cap, 2 * cut + 128)
        lasts = rows[:, 2 * cut :]
        for p, w in enumerate((wg, wu, wd)):
            lo = 0 if p < 2 else cut
            got = mm(rows[:, lo : lo + cut], w[0:cut, :]) + mm(lasts, w[cut:full, :])
            part[s, p] = got.astype(bf16)
            pair_copy(s, p).start()

    def second(s):
        for p in range(3):
            pair_copy(s, p).wait_recv()
            at = pl.ds(mine, half)
            part[s, p, at] = (part[s, p, at].astype(f32) + precv[s, p].astype(f32)).astype(bf16)
        for i in range(3):
            sum_copy(s, i).start()

    def third(s):
        total = part[s, :, pl.ds(pl.multiple_of(mine + y * cap, cap), cap)].astype(f32)
        for i in range(3):
            sum_copy(s, i).wait_recv()
            total = total + rsum[s, i].astype(f32)
        gate, upv, back = total[0], total[1], total[2]
        sigma = 1.0 / (1.0 + jnp.exp(-gate))
        at = pl.ds(pl.multiple_of(mine + y * cap, cap), cap)
        gall[s, at, 0:hidden] = (back * upv * sigma * (1.0 + gate * (1.0 - sigma))).astype(bf16)
        gall[s, at, hidden : 2 * hidden] = (back * gate * sigma).astype(bf16)
        for i in range(3):
            grad_copy(s, i, y).start()
        fwd_copy(s, 3, k, y).start()

    def fourth(s):
        for i in range(3):
            grad_copy(s, i, froms[i]).wait_recv()
            fwd_copy(s, i, k, froms[i]).start()

    def fifth(s):
        for i in range(3):
            fwd_copy(s, i, 1 - k, froms[i]).wait_recv()
        fwd_copy(s, 3, 1 - k, y).wait_recv()
        grad = mm(gall[s, :, 0:hidden], wg[0:cols, :], 1, 1) + mm(
            gall[s, :, hidden : 2 * hidden], wu[0:cols, :], 1, 1
        )
        eg[s] = grad.astype(bf16).reshape(nz, cap, cols)

        def one(i, _):
            @pl.when(s * nz + i > 0)
            def _():
                back_copy(s, i).start()

            return 0

        lax.fori_loop(0, nz, one, 0)

    def back_copy(s, i):
        return remote(
            eg.at[s, i],
            ret.at[me],
            rsem.at[0, s * nz + i],
            rsem.at[1, s * nz + i],
            "ctx",
            behind(s, i),
        )

    def stage(s, _):
        first(s)

        @pl.when(s + 2 < nx)
        def _():
            lax.fori_loop((s + 2) * nz, (s + 3) * nz, post, 0)

        second(s)

        @pl.when(s > 0)
        def _():
            fourth(s - 1)
            fifth(s - 1)

        third(s)
        return 0

    lax.fori_loop(0, nx, stage, 0)
    totals("start")
    exchange(n, me, st_send, st_recv, sem_s.at[0], sem_s.at[1], "start")
    st_recv[me] = st_send[me]
    tot_ref[me] = tot_send[...]
    fourth(nx - 1)
    w_hop(1)
    fifth(nx - 1)
    w_hop(2)
    ret[me] = eg[0, 0]

    def finish(i, _):
        dx, dz = i // nz, lax.rem(i, nz)
        it = ahead(dx, dz)
        remote(eg.at[dx, dz], ret.at[it], rsem.at[0, i], rsem.at[1, i], "ctx", it).wait_recv()
        return 0

    lax.fori_loop(1, n, finish, 0)
    entries = ret[...].reshape(slots, cols)
    input_grad = g_ref[...].astype(f32) + mm(entries, pick[...], 0, 0)
    ya[y] = input_grad.reshape(nz // 2, cols // (nz // 2), tok).astype(bf16)

    def y_copy(i, chunk):
        return remote(
            ya.at[chunk], ya.at[chunk], ysem.at[0, i], ysem.at[1, i], "tp", (up, dn, op)[i]
        )

    def x_copy(chunk, source):
        return remote(
            ya.at[chunk],
            xa.at[source, k],
            xsem.at[0, chunk],
            xsem.at[1, source],
            "ctx",
            chunk * nz + z,
        )

    def f_copy(source, core):
        at = xa.at[source, core]
        return remote(at, at, hfsem.at[0, source], hfsem.at[1, source], "tp", sib)

    def pass_on(chunk):
        @pl.when(chunk != x)
        def _():
            x_copy(chunk, x).start()

        @pl.when(chunk == x)
        def _():
            xa[x, k] = ya[chunk]
            f_copy(x, k).start()

    for i in range(3):
        y_copy(i, y).start()
    pass_on(y)
    out_ref[...] = input_grad.astype(bf16)
    w_hop(3)
    for i in range(3):
        y_copy(i, froms[i]).wait_recv()
        pass_on(froms[i])

    totals("wait")
    exchange(n, me, st_send, st_recv, sem_s.at[0], sem_s.at[1], "wait")
    size = width // heads
    scan_states(n, me, st_recv, back_send, tot_ref, size, False)
    exchange(n, me, back_send, before_ref, sem_b.at[0], sem_b.at[1], "start")
    before_ref[me] = back_send[me]

    def x_at(d):
        return lax.rem(x + d, nx)

    def product(source):
        total = jnp.zeros((tok, width), f32)
        for b in range(nz):
            total = total + mm(xa[source, b // (nz // 2), b % (nz // 2)], w[b], 0, 0)
        return total

    def h_copy(d):
        return remote(
            hsend.at[d - 1],
            hrecv.at[d - 1],
            hsem.at[0, d - 1],
            hsem.at[1, d - 1],
            "ctx",
            x_at(d) * nz + z,
        )

    order = [1, nx - 1] + list(range(2, nx - 1))
    for d in order:
        source = x_at(d)
        x_copy(x, source).wait_recv()
        f_copy(source, k).start()
    w_landed(3)
    for d in order:
        source = x_at(d)
        f_copy(source, 1 - k).wait_recv()
        hsend[d - 1] = product(source).astype(bf16)
        h_copy(d).start()
    f_copy(x, 1 - k).wait_recv()
    whole = product(x)
    for d in order:
        h_copy(d).wait_recv()
        whole = whole + hrecv[d - 1].astype(f32)

    grad = whole.astype(bf16)
    ge = (grad.astype(f32) * er_ref[...]).astype(bf16)
    gst_send[...] = mm(ge, c_ref[...], 0, 0).astype(bf16).reshape(gst_send.shape)
    exchange(n, me, gst_send, gst_recv, gsem_s.at[0], gsem_s.at[1], "start")
    gst_recv[me] = gst_send[me]

    weights = jnp.zeros((tok, tok), f32)
    for h in range(heads):
        gh = grad[:, h * size : (h + 1) * size]
        uh = u_ref[:, h * size : (h + 1) * size]
        weights = weights + decay_ref[h].astype(f32) * mm(gh, uh, 1, 1)
        intra[:, h * size : (h + 1) * size] = mm(mix_ref[h], gh, 0, 0)
    weights = weights.astype(bf16)
    state = b_ref.shape[1]

    exchange(n, me, gst_send, gst_recv, gsem_s.at[0], gsem_s.at[1], "wait")
    scan_states(n, me, gst_recv, gback_send, tot_ref, size, True)
    exchange(n, me, gback_send, after, gsem_b.at[0], gsem_b.at[1], "start")
    after[me] = gback_send[me]

    exchange(n, me, back_send, before_ref, sem_b.at[0], sem_b.at[1], "wait")
    out_map_ref[...] = mm(weights, b_ref[...]) + mm(ge, before_ref[...].reshape(-1, state))
    in_part = mm(weights, c_ref[...], 0, 0)

    def settle(s, _):
        for p in range(3):
            pair_copy(s, p).wait_send()
        for i in range(3):
            sum_copy(s, i).wait_send()
            grad_copy(s, i, y).wait_send()
            fwd_copy(s, i, k, froms[i]).wait_send()
        fwd_copy(s, 3, k, y).wait_send()
        return 0

    lax.fori_loop(0, nx, settle, 0)

    def sent(i, _):
        dx, dz = i // nz, lax.rem(i, nz)
        it = ahead(dx, dz)
        remote(
            send.at[it], inbuf.at[dx, dz], isem.at[0, i], isem.at[1, i], "ctx", it
        ).wait_send()
        remote(eg.at[dx, dz], ret.at[it], rsem.at[0, i], rsem.at[1, i], "ctx", it).wait_send()
        return 0

    lax.fori_loop(1, n, sent, 0)
    for j in range(nz // 2):
        w_copy(j, True).wait_send()
        w_copy(j, False).wait_send()
    for i in range(3):
        y_copy(i, y).wait_send()
    for d in order:
        x_copy(x_at(d), x).wait_send()
        h_copy(d).wait_send()
    for d in range(nx):
        f_copy(x_at(d), k).wait_send()

    exchange(n, me, gback_send, after, gsem_b.at[0], gsem_b.at[1], "wait")
    later = after[...].reshape(-1, state)
    in_ref[...] = in_part + mm(ut_ref[...], later)
    scan_ref[...] = (intra[...] + tail_ref[...] * mm(b_ref[...], later, 1, 1)).astype(bf16)


def layer(
    sizes, moe_t, grad_t, ids_t, prob_t, counts, ssd_input, in_map, out_map, log_t, wg, wu, wd, w
):
    nx, nz, ny = sizes
    n = nx * nz
    cols, tok = moe_t.shape
    experts = counts.shape[1]
    cap = 2 * tok * ids_t.shape[0] // experts
    heads = log_t.shape[0]
    width = ssd_input.shape[1]
    state = in_map.shape[1]
    hidden = wg.shape[1]
    part = width // n
    cut = cols // 128 * 128
    full = cut + 128
    rows = nz * cap
    small = jax.ShapeDtypeStruct((tok, state), f32)
    states = pltpu.VMEM((n, part, state), bf16)
    pairs = DMA((2, n))
    return pl.pallas_call(
        functools.partial(layer_kernel, nx, nz, ny),
        out_shape=(
            jax.ShapeDtypeStruct((cols, tok), bf16),
            jax.ShapeDtypeStruct((tok, width), bf16),
            small,
            small,
        ),
        in_specs=[VMEM] * 9 + [ANY] * 4,
        out_specs=[VMEM] * 4,
        scratch_shapes=[
            pltpu.VMEM((tok, width), f32),
            pltpu.VMEM((tok, width), f32),
            pltpu.VMEM((tok, width), bf16),
            pltpu.VMEM((heads, tok, tok), bf16),
            pltpu.VMEM((heads, tok, tok), bf16),
            states,
            pltpu.VMEM((n, 8, 128), f32),
            pltpu.VMEM((full, hidden), bf16),
            pltpu.VMEM((full, hidden), bf16),
            pltpu.VMEM((full, hidden), bf16),
            pltpu.VMEM((n, cap, 2 * cut + 128), bf16),
            pltpu.VMEM((nx, nz, cap, 2 * cut + 128), bf16),
            pltpu.VMEM((nx, 3, rows, hidden), bf16),
            pltpu.VMEM((nx, 3, rows // 2, hidden), bf16),
            pltpu.VMEM((nx, 3, 3, cap, hidden), bf16),
            pltpu.VMEM((nx, rows, 2 * hidden), bf16),
            pltpu.VMEM((nx, nz, cap, cols), bf16),
            pltpu.VMEM((n, cap, cols), bf16),
            pltpu.VMEM((experts * cap, tok), bf16),
            states,
            states,
            states,
            pltpu.VMEM((8, 128), f32),
            pltpu.VMEM((nz, w.shape[0], width), bf16),
            pltpu.VMEM((ny, nz // 2, w.shape[0], tok), bf16),
            pltpu.VMEM((nx, 2, nz // 2, w.shape[0], tok), bf16),
            pltpu.VMEM((nx - 1, tok, width), bf16),
            pltpu.VMEM((nx - 1, tok, width), bf16),
            pltpu.VMEM((tok, width), f32),
            states,
            states,
            states,
            states,
            DMA((5,)),
            pairs,
            DMA((2, nx, 3)),
            DMA((2, nx, 3)),
            DMA((2, nx, 3)),
            DMA((2, nx, 4)),
            pairs,
            pairs,
            pairs,
            pairs,
            DMA((2, nz // 2)),
            DMA((2, nz // 2)),
            DMA((2, 3)),
            DMA((2, nx)),
            DMA((2, nx)),
            DMA((2, nx - 1)),
            pairs,
            pairs,
        ],
        compiler_params=pltpu.CompilerParams(
            collective_id=0, has_side_effects=True, vmem_limit_bytes=46 * 2**20
        ),
        name="layer",
    )(moe_t, grad_t, ids_t, prob_t, counts, ssd_input, in_map, out_map, log_t, wg, wu, wd, w)


def body(
    moe_input,
    out_grad,
    route_prob,
    route_ids,
    route_counts,
    w_gate,
    w_up,
    w_down,
    out_weight,
    ssd_input,
    input_map,
    output_map,
    log_decay,
):
    n = lax.axis_size("ctx")
    ny = lax.axis_size("tp") // 2
    nx = ny
    nz = n // nx
    grad_t, scan_grad, in_map_grad, out_map_grad = layer(
        (nx, nz, ny),
        moe_input.T,
        out_grad.T,
        route_ids.T,
        route_prob.T,
        route_counts,
        ssd_input,
        input_map,
        output_map,
        log_decay.T,
        w_gate[0],
        w_up[0],
        w_down[0].T,
        out_weight,
    )
    return (grad_t.T, scan_grad, in_map_grad, out_map_grad)


def solution(mesh):
    in_specs = (
        P("ctx", "tp"),
        P("ctx", "tp"),
        P("ctx", None),
        P("ctx", None),
        P("ctx", None),
        P("ctx", "tp", None),
        P("ctx", "tp", None),
        P("ctx", None, "tp"),
        P("ctx", "tp"),
        P("ctx", "tp"),
        P("ctx", "tp"),
        P("ctx", "tp"),
        P("ctx", "tp"),
    )
    out_specs = (P("ctx", "tp"), P("ctx", "tp"), P("ctx", "tp"), P("ctx", "tp"))
    return jax.shard_map(body, mesh=mesh, in_specs=in_specs, out_specs=out_specs, check_vma=False)
```

time: 627 us -> 195 us (0.31)
  waiting for transfers between devices: 426 us -> 0 us
  Pallas kernels: 0 us -> 178 us
  other arithmetic: 63.1 us -> 0 us
  matrix products: 37.2 us -> 0 us
  blocking collectives: 32.3 us -> 0 us
  starting transfers between devices: 30.7 us -> 0 us
  between operations: 14.1 us -> 0.67 us
    all_gather x4 -> x0, waiting for transfers between devices: 298 us -> none  [the longest x2 149 us: entering(): lax.all_gather(a.astype(kind), axis)]
    pallas_call x0 -> x1, Pallas kernels: none -> 178 us  [layer(): pl.pallas_call(functools.partial(layer_kernel, nx, nz, ny), out_shape=(ja...]
    psum x1 -> x0, waiting for transfers between devices: 79.2 us -> none  [body(): lax.psum(gate_part.astype(jnp.bfloat16), 'tp').astype(jnp.float32)]
    all_to_all x3 -> x0, waiting for transfers between devices: 47.1 us -> none  [the longest x1 19.4 us: body(): lax.all_to_all(returned, 'ctx', split_axis=0, concat_axis=0, tiled=True)]
    dot_general x16 -> x0, matrix products: 37.2 us -> none  [the longest x1 7.12 us: body(): jnp.dot(full_grad, lax.all_gather(out_weight, 'ctx', axis=0, tiled=True),...]
    add x31 -> x0, other arithmetic: 34.2 us -> none  [chain_combine(): later[1] + later[0][:, None, None] * earlier[1]]
    all_gather x1 -> x0, blocking collectives: 32.3 us -> none  [entering(): lax.all_gather(a.astype(kind), axis)]
    all_to_all x3 -> x0, starting transfers between devices: 30.1 us -> none  [the longest x1 12.1 us: body(): lax.all_to_all(send_rows, 'ctx', split_axis=0, concat_axis=0, tiled=True)]
  transfers between devices with their start and end apart: 8 -> 0, of which waited for: 8 -> 0; matrix products, arithmetic and copies ran while one was open for 5% -> 0% of each run, Pallas kernels for 0% -> 0%
where the time goes in v2:
time: 195 us; the launch traced here: 193 us
  Pallas kernels  178 us (91%)
  local copies, waits for them, and re-layouts  14.1 us (7%)
    pallas_call x1, Pallas kernels, layer(): pl.pallas_call(functools.partial(layer_kernel, nx, nz, ny), out_shape=(ja...  178 us
    unnamed x28, local copies, waits for them, and re-layouts  14.1 us

profile of v2, /device:TPU:1, one launch (start us, length us, event | category | flops | bytes accessed | tf_op | source)
XLA Modules:
  0.0 193.2 jit_solution(1685467701999013188)
XLA Ops:
  0.6 0.0 copy-start
  0.6 1.7 copy-done
  2.3 0.0 copy-start.1
  2.3 1.7 copy-done.1
  4.0 0.0 copy-start.2
  4.0 1.0 copy-done.2
  5.0 0.0 copy-start.3
  5.0 0.9 copy-done.3
  6.0 0.0 copy-start.4
  6.0 0.9 copy-done.4
  6.9 0.0 copy-start.5
  6.9 0.9 copy-done.5
  7.8 0.0 copy-start.6
  7.8 0.8 copy-done.6
  8.6 0.0 copy-start.7
  8.6 0.8 copy-done.7
  9.4 0.0 copy-start.8
  9.4 0.7 copy-done.8
  10.1 0.0 copy-start.9
  10.1 0.7 copy-done.9
  10.7 0.0 copy-start.10
  10.7 0.7 copy-done.10
  11.4 0.0 copy-start.11
  11.4 0.7 copy-done.11
  12.1 178.4 %layer.1 = (bf16[800,128]{1,0:T(8,128)(2,1)S(1)}, bf16[128,1024]{1,0:T(8,128)(2,1)S(1)}, f32[128,128]{1,0:T(8,128)S(1)}, f32[128,128]{1,0:T(8,128)S(1)}) custom-call(bf16[800,128]{1,0:T(8,128)(2,1)S(1)} %bitcast.14, bf16[800,128]{1,0:T(8,128)(2,1)S(1)} %bitcast.15, s32[2,128]{1,0:T(2,128)S(1)} %bitcast.17, f32[2,128]{1,0:T(2,128)S(1)} %bitcast.18, ...), custom_call_target="tpu_custom_call" | custom-call | tf_op jit(solution)/shard_map/layer/pallas_call | solution.py:649
  190.5 0.7 copy.21
  191.2 0.7 copy.22
  191.9 0.6 copy.23
  192.5 0.6 copy.24
Async XLA Ops:
  0.6 1.7 copy-start
  2.3 1.7 copy-start.1
  4.0 1.0 copy-start.2
  5.0 0.9 copy-start.3
  6.0 0.9 copy-start.4
  6.9 0.9 copy-start.5
  7.8 0.8 copy-start.6
  8.6 0.8 copy-start.7
  9.4 0.7 copy-start.8
  10.1 0.7 copy-start.9
  10.7 0.7 copy-start.10
  11.4 0.7 copy-start.11

commit v3 on v2

--- a/solution.py
+++ b/solution.py
@@ -11,7 +11,7 @@
 HIGHEST = lax.Precision.HIGHEST
 bf16, f32, i32 = jnp.bfloat16, jnp.float32, jnp.int32
 VMEM = pl.BlockSpec(memory_space=pltpu.VMEM)
-ANY = pl.BlockSpec(memory_space=pl.ANY)
+HBM = pl.BlockSpec(memory_space=pltpu.HBM)
 DMA = pltpu.SemaphoreType.DMA
 
 
@@ -74,8 +74,8 @@
     return mm(columns, put.astype(f32), precision=HIGHEST)
 
 
-def scan_states(n, me, loc, out, totals, rows_per_head, backward):
-    head = me * loc.shape[1] // rows_per_head
+def scan_states(n, me, loc, out, totals, rows_per_head, first_head, backward):
+    head = first_head + me * loc.shape[1] // rows_per_head
     lane = lax.broadcasted_iota(i32, totals.shape, 2)
     decay = jnp.exp(jnp.sum(jnp.where(lane == head, totals[...], 0.0), axis=2, keepdims=True))
     state = jnp.zeros(loc.shape[1:], f32)
@@ -89,6 +89,23 @@
     nx,
     nz,
     ny,
+    x_hbm,
+    g_hbm,
+    ids_hbm,
+    prob_hbm,
+    counts_hbm,
+    u_hbm,
+    b_hbm,
+    c_hbm,
+    ld_hbm,
+    wg_hbm,
+    wu_hbm,
+    wd_hbm,
+    w_hbm,
+    out_ref,
+    scan_ref,
+    in_ref,
+    out_map_ref,
     x_ref,
     g_ref,
     ids_ref,
@@ -98,14 +115,6 @@
     b_ref,
     c_ref,
     ld_ref,
-    wg_hbm,
-    wu_hbm,
-    wd_hbm,
-    w_hbm,
-    out_ref,
-    scan_ref,
-    in_ref,
-    out_map_ref,
     er_ref,
     tail_ref,
     ut_ref,
@@ -157,6 +166,7 @@
     hsem,
     gsem_s,
     gsem_b,
+    lsem,
 ):
     n = nx * nz
     me = lax.axis_index("ctx")
@@ -165,7 +175,7 @@
     y, k = t // 2, lax.rem(t, 2)
     sib = y * 2 + (1 - k)
     y_up, y_dn, y_op = lax.rem(y + 1, ny), lax.rem(y + ny - 1, ny), lax.rem(y + 2, ny)
-    up, dn, op = y_up * 2 + k, y_dn * 2 + k, y_op * 2 + k
+    up, dn = y_up * 2 + k, y_dn * 2 + k
 
     def ahead(dx, dz):
         return lax.rem(x + dx, nx) * nz + lax.rem(z + dz, nz)
@@ -173,7 +183,22 @@
     def behind(dx, dz):
         return lax.rem(x - dx + nx, nx) * nz + lax.rem(z - dz + nz, nz)
 
-    cols, tok = x_ref.shape
+    def offset(s, i):
+        j = i // nx
+        dz = jnp.where(j == 0, s + 1, jnp.where(s == nz // 2 - 1, 0, nz - 1 - s))
+        return lax.rem(i, nx), dz
+
+    def target(s, i):
+        return ahead(*offset(s, i))
+
+    def origin(s, i):
+        return behind(*offset(s, i))
+
+    per = 2 * nx
+    stages = nz // 2
+    own = (stages - 1, nx)
+
+    cols, tok = x_hbm.shape
     hidden = wg.shape[1]
     cut = wd_hbm.shape[0] // 128 * 128
     loads = [
@@ -184,12 +209,32 @@
             wd_hbm.at[pl.ds(cut, cols - cut)], wd.at[pl.ds(cols, cols - cut)], wsem.at[3]
         ),
     ]
+    small = [
+        pltpu.make_async_copy(src, dst, lsem.at[i])
+        for i, (src, dst) in enumerate(
+            (
+                (ids_hbm, ids_ref),
+                (counts_hbm, counts_ref),
+                (x_hbm, x_ref),
+                (g_hbm, g_ref),
+                (prob_hbm, prob_ref),
+                (ld_hbm, ld_ref),
+                (u_hbm, u_ref),
+                (b_hbm, b_ref),
+                (c_hbm, c_ref),
+            )
+        )
+    ]
+    for load in small:
+        load.start()
     own_w = pltpu.make_async_copy(w_hbm, w.at[z], wsem.at[4])
     own_w.start()
     for load in loads:
         load.start()
     hello_ctx(n, me)
-    hello_tp((sib, up, dn, op))
+    hello_tp((sib, up, dn))
+    for load in small[0:2]:
+        load.wait()
 
     experts = counts_ref.shape[1]
     cap = inbuf.shape[2]
@@ -216,7 +261,7 @@
     both = (p0 + p1).astype(bf16)
     pick[...] = both
 
-    pl.semaphore_wait(pltpu.get_barrier_semaphore(), n - 1 + 4)
+    pl.semaphore_wait(pltpu.get_barrier_semaphore(), n - 1 + 3)
     mid = w.shape[2] // 2
     last_hop = nz // 2 - 1
 
@@ -246,8 +291,8 @@
         w_copy(j, True).start()
         w_copy(j, False).start()
 
-    own_w.wait()
-    w_hop(0)
+    for load in small[2:]:
+        load.wait()
     grad = g_ref[...].astype(f32)
     prob = prob_ref[...]
     scaled = jnp.concatenate(
@@ -263,16 +308,24 @@
     )
     send[:, :, 2 * cut :] = last.astype(bf16).reshape(experts, cap, 128)
 
+    def in_copy(s, j):
+        to = target(s, j)
+        at = s * per + j
+        return remote(
+            send.at[to], inbuf.at[s, j], isem.at[0, at], isem.at[1, at], "ctx", to
+        )
+
     def post(i, _):
-        dx, dz = i // nz, lax.rem(i, nz)
-        to = ahead(dx, dz)
-        remote(
-            send.at[to], inbuf.at[dx, dz], isem.at[0, i], isem.at[1, i], "ctx", to
-        ).start()
+        s, j = i // per, lax.rem(i, per)
+
+        @pl.when(i != own[0] * per + own[1])
+        def _():
+            in_copy(s, j).start()
+
         return 0
 
-    lax.fori_loop(1, 2 * nz, post, 0)
-    inbuf[0, 0] = send[me]
+    lax.fori_loop(0, per, post, 0)
+    inbuf[own] = send[me]
 
     heads = ld_ref.shape[0]
     width = u_ref.shape[1]
@@ -328,7 +381,7 @@
         decay_ref[h] = decay.astype(bf16)
         mix_ref[h] = (decay * affinity).astype(bf16)
 
-    half = nz // 2 * cap
+    half = per // 2 * cap
     mine, other = pl.multiple_of(k * half, cap), pl.multiple_of((1 - k) * half, cap)
 
     def pair_copy(s, p):
@@ -341,15 +394,23 @@
             sib,
         )
 
+    side = hidden // 2
+    lows, highs = pl.ds(0, side), pl.ds(side, side)
+
+    def chunk(dz):
+        return pl.ds(pl.multiple_of(mine + dz * cap, cap), cap)
+
     def sum_copy(s, i):
-        to, dz = ((up, y_up), (dn, y_dn), (op, y_op))[i]
+        src = (
+            part.at[s, :, chunk(y_op), lows],
+            part.at[s, :, chunk(y_op), highs],
+            part.at[s, :, chunk(y_up), highs],
+            part.at[s, :, chunk(y_dn), lows],
+            rsum.at[s, 6],
+            rsum.at[s, 7],
+        )[i]
         return remote(
-            part.at[s, :, pl.ds(pl.multiple_of(mine + dz * cap, cap), cap)],
-            rsum.at[s, i],
-            ssem.at[0, s, i],
-            ssem.at[1, s, i],
-            "tp",
-            to,
+            src, rsum.at[s, i], ssem.at[0, s, i], ssem.at[1, s, i], "tp", (up, dn)[i % 2]
         )
 
     def grads_at(s, core, dz):
@@ -358,8 +419,10 @@
     froms = (y_dn, y_up, y_op)
 
     def grad_copy(s, i, dz):
-        at = grads_at(s, k, dz)
-        return remote(at, at, gsem.at[0, s, i], gsem.at[1, s, i], "tp", (up, dn, op)[i])
+        at = gall.at[s, chunk(dz)]
+        if i >= 2:
+            at = gall.at[s, chunk(dz), pl.ds((i - 2) * hidden, hidden)]
+        return remote(at, at, gsem.at[0, s, i], gsem.at[1, s, i], "tp", (up, dn)[i % 2])
 
     def fwd_copy(s, i, core, dz):
         at = grads_at(s, core, dz)
@@ -367,21 +430,18 @@
 
     def first(s):
         def one(i, _):
-            @pl.when(s * nz + i > 0)
+            @pl.when(jnp.logical_and(i == per // 2, jnp.logical_and(s != 1, s + 1 < stages)))
             def _():
-                remote(
-                    send.at[ahead(s, i)],
-                    inbuf.at[s, i],
-                    isem.at[0, s * nz + i],
-                    isem.at[1, s * nz + i],
-                    "ctx",
-                    ahead(s, i),
-                ).wait_recv()
+                lax.fori_loop((s + 1) * per, (s + 2) * per, post, 0)
+
+            @pl.when(s * per + i != own[0] * per + own[1])
+            def _():
+                in_copy(s, i).wait_recv()
 
             return 0
 
-        lax.fori_loop(0, nz, one, 0)
-        rows = inbuf[s].reshape(nz * cap, 2 * cut + 128)
+        lax.fori_loop(0, per, one, 0)
+        rows = inbuf[s].reshape(per * cap, 2 * cut + 128)
         lasts = rows[:, 2 * cut :]
         for p, w in enumerate((wg, wu, wd)):
             lo = 0 if p < 2 else cut
@@ -394,27 +454,45 @@
             pair_copy(s, p).wait_recv()
             at = pl.ds(mine, half)
             part[s, p, at] = (part[s, p, at].astype(f32) + precv[s, p].astype(f32)).astype(bf16)
-        for i in range(3):
+        for i in range(4):
             sum_copy(s, i).start()
 
+    def relay(s):
+        for i, (dz, at) in enumerate(((y_up, lows), (y_dn, highs))):
+            sum_copy(s, i).wait_recv()
+            rsum[s, 6 + i] = (
+                part[s, :, chunk(dz), at].astype(f32) + rsum[s, i].astype(f32)
+            ).astype(bf16)
+            sum_copy(s, 4 + i).start()
+
     def third(s):
-        total = part[s, :, pl.ds(pl.multiple_of(mine + y * cap, cap), cap)].astype(f32)
-        for i in range(3):
+        for i in range(2, 6):
             sum_copy(s, i).wait_recv()
-            total = total + rsum[s, i].astype(f32)
-        gate, upv, back = total[0], total[1], total[2]
-        sigma = 1.0 / (1.0 + jnp.exp(-gate))
-        at = pl.ds(pl.multiple_of(mine + y * cap, cap), cap)
-        gall[s, at, 0:hidden] = (back * upv * sigma * (1.0 + gate * (1.0 - sigma))).astype(bf16)
-        gall[s, at, hidden : 2 * hidden] = (back * gate * sigma).astype(bf16)
-        for i in range(3):
+        for e, at, near, far in ((0, lows, 3, 4), (1, highs, 2, 5)):
+            total = (
+                part[s, :, chunk(y), at].astype(f32)
+                + rsum[s, near].astype(f32)
+                + rsum[s, far].astype(f32)
+            )
+            gate, upv, back = total[0], total[1], total[2]
+            sigma = 1.0 / (1.0 + jnp.exp(-gate))
+            lo, hi = pl.ds(e * side, side), pl.ds(hidden + e * side, side)
+            gall[s, chunk(y), lo] = (back * upv * sigma * (1.0 + gate * (1.0 - sigma))).astype(bf16)
+            gall[s, chunk(y), hi] = (back * gate * sigma).astype(bf16)
+        for i in range(2):
             grad_copy(s, i, y).start()
         fwd_copy(s, 3, k, y).start()
 
     def fourth(s):
-        for i in range(3):
+        for i in range(2):
             grad_copy(s, i, froms[i]).wait_recv()
+            grad_copy(s, 2 + i, froms[i]).start()
             fwd_copy(s, i, k, froms[i]).start()
+
+    def gathered(s):
+        for i in range(2):
+            grad_copy(s, 2 + i, y_op).wait_recv()
+        fwd_copy(s, 2, k, y_op).start()
 
     def fifth(s):
         for i in range(3):
@@ -423,208 +501,294 @@
         grad = mm(gall[s, :, 0:hidden], wg[0:cols, :], 1, 1) + mm(
             gall[s, :, hidden : 2 * hidden], wu[0:cols, :], 1, 1
         )
-        eg[s] = grad.astype(bf16).reshape(nz, cap, cols)
+        eg[s] = grad.astype(bf16).reshape(per, cap, cols)
 
         def one(i, _):
-            @pl.when(s * nz + i > 0)
+            @pl.when(s * per + i != own[0] * per + own[1])
             def _():
                 back_copy(s, i).start()
 
             return 0
 
-        lax.fori_loop(0, nz, one, 0)
+        lax.fori_loop(0, per, one, 0)
 
     def back_copy(s, i):
+        at = s * per + i
         return remote(
-            eg.at[s, i],
-            ret.at[me],
-            rsem.at[0, s * nz + i],
-            rsem.at[1, s * nz + i],
-            "ctx",
-            behind(s, i),
-        )
+            eg.at[s, i], ret.at[me], rsem.at[0, at], rsem.at[1, at], "ctx", origin(s, i)
+        )
+
+    def back_landed(s, i):
+        at, it = s * per + i, target(s, i)
+        return remote(eg.at[s, i], ret.at[it], rsem.at[0, at], rsem.at[1, at], "ctx", it)
 
     def stage(s, _):
-        first(s)
-
-        @pl.when(s + 2 < nx)
-        def _():
-            lax.fori_loop((s + 2) * nz, (s + 3) * nz, post, 0)
-
         second(s)
 
         @pl.when(s > 0)
         def _():
             fourth(s - 1)
+
+        @pl.when(s > 1)
+        def _():
+            fifth(s - 2)
+
+        relay(s)
+
+        @pl.when(s == 0)
+        def _():
+            lax.fori_loop(2 * per, 3 * per, post, 0)
+
+        @pl.when(s > 0)
+        def _():
+            gathered(s - 1)
+
+        @pl.when(s + 1 < stages)
+        def _():
+            first(s + 1)
+
+        @pl.when(s == stages - 2)
+        def _():
+            w_hop(0)
+
+        @pl.when(s == stages - 1)
+        def _():
             fifth(s - 1)
 
         third(s)
         return 0
 
-    lax.fori_loop(0, nx, stage, 0)
+    own_w.wait()
+    first(0)
+    lax.fori_loop(0, stages, stage, 0)
+    fourth(stages - 1)
+    w_hop(1)
+    gathered(stages - 1)
+    fifth(stages - 1)
+    ret[me] = eg[own]
+
+    def each(act):
+        def one(i, _):
+            @pl.when(i != own[0] * per + own[1])
+            def _():
+                act(i // per, lax.rem(i, per))
+
+            return 0
+
+        lax.fori_loop(0, n, one, 0)
+
+    each(lambda a, b: back_landed(a, b).wait_recv())
+    w_hop(2)
+    entries = ret[...].reshape(slots, cols)
+    input_grad = g_ref[...].astype(f32) + mm(entries, pick[...], 0, 0)
+    ya[y] = input_grad.reshape(nz // 2, cols // (nz // 2), tok).astype(bf16)
+
+    def y_copy(i, dz):
+        at = ya.at[dz]
+        if i >= 2:
+            at = ya.at[dz, pl.ds((i - 2) * (nz // 4), nz // 4)]
+        return remote(at, at, ysem.at[0, i], ysem.at[1, i], "tp", (up, dn)[i % 2])
+
+    def x_copy(place, source):
+        return remote(
+            ya.at[place],
+            xa.at[source, k],
+            xsem.at[0, place],
+            xsem.at[1, source],
+            "ctx",
+            place * nz + z,
+        )
+
+    def f_copy(source, core):
+        at = xa.at[source, core]
+        return remote(at, at, hfsem.at[0, source], hfsem.at[1, source], "tp", sib)
+
+    def pass_on(place):
+        @pl.when(place != x)
+        def _():
+            x_copy(place, x).start()
+
+        @pl.when(place == x)
+        def _():
+            xa[x, k] = ya[place]
+            f_copy(x, k).start()
+
+    for i in range(2):
+        y_copy(i, y).start()
+    pass_on(y)
+    out_ref[...] = input_grad.astype(bf16)
+    for i in range(2):
+        y_copy(i, froms[i]).wait_recv()
+        y_copy(2 + i, froms[i]).start()
+        pass_on(froms[i])
+    for i in range(2):
+        y_copy(2 + i, y_op).wait_recv()
+    pass_on(y_op)
+
+    def x_at(d):
+        return lax.rem(x + d, nx)
+
+    wide = width // 2
+    quarter = wide // 2
+
+    def product(source, hf):
+        total = jnp.zeros((tok, wide), f32)
+        for b in range(nz):
+            part_x = xa[source, b // (nz // 2), b % (nz // 2)]
+            total = total + mm(part_x, w[b, :, pl.ds(hf * wide, wide)], 0, 0)
+        return total
+
+    x_up, x_dn, x_op = x_at(1), x_at(nx - 1), x_at(2)
+    def quart(hf, q):
+        return pl.ds(hf * wide + q * quarter, quarter)
+
+    def h_copy(hf, i):
+        src, q = ((0, 0), (0, 1), (1, 1), (2, 0), (1, 0), (2, 1))[i]
+        return remote(
+            hsend.at[src, :, quart(hf, q)],
+            hrecv.at[hf, i],
+            hsem.at[0, hf, i],
+            hsem.at[1, hf, i],
+            "ctx",
+            (x_up, x_dn)[i % 2] * nz + z,
+        )
+
+    order = [2, 1, nx - 1]
+    w_hop(3)
+    for d in order:
+        source = x_at(d)
+        x_copy(x, source).wait_recv()
+        f_copy(source, k).start()
     totals("start")
     exchange(n, me, st_send, st_recv, sem_s.at[0], sem_s.at[1], "start")
     st_recv[me] = st_send[me]
     tot_ref[me] = tot_send[...]
-    fourth(nx - 1)
-    w_hop(1)
-    fifth(nx - 1)
-    w_hop(2)
-    ret[me] = eg[0, 0]
-
-    def finish(i, _):
-        dx, dz = i // nz, lax.rem(i, nz)
-        it = ahead(dx, dz)
-        remote(eg.at[dx, dz], ret.at[it], rsem.at[0, i], rsem.at[1, i], "ctx", it).wait_recv()
-        return 0
-
-    lax.fori_loop(1, n, finish, 0)
-    entries = ret[...].reshape(slots, cols)
-    input_grad = g_ref[...].astype(f32) + mm(entries, pick[...], 0, 0)
-    ya[y] = input_grad.reshape(nz // 2, cols // (nz // 2), tok).astype(bf16)
-
-    def y_copy(i, chunk):
-        return remote(
-            ya.at[chunk], ya.at[chunk], ysem.at[0, i], ysem.at[1, i], "tp", (up, dn, op)[i]
-        )
-
-    def x_copy(chunk, source):
-        return remote(
-            ya.at[chunk],
-            xa.at[source, k],
-            xsem.at[0, chunk],
-            xsem.at[1, source],
-            "ctx",
-            chunk * nz + z,
-        )
-
-    def f_copy(source, core):
-        at = xa.at[source, core]
-        return remote(at, at, hfsem.at[0, source], hfsem.at[1, source], "tp", sib)
-
-    def pass_on(chunk):
-        @pl.when(chunk != x)
-        def _():
-            x_copy(chunk, x).start()
-
-        @pl.when(chunk == x)
-        def _():
-            xa[x, k] = ya[chunk]
-            f_copy(x, k).start()
-
-    for i in range(3):
-        y_copy(i, y).start()
-    pass_on(y)
-    out_ref[...] = input_grad.astype(bf16)
-    w_hop(3)
-    for i in range(3):
-        y_copy(i, froms[i]).wait_recv()
-        pass_on(froms[i])
-
+    size = width // heads
+    w_landed(3)
+    for hf in range(2):
+        for i, d in enumerate(order):
+            source = x_at(d)
+            if hf == 0:
+                f_copy(source, 1 - k).wait_recv()
+            hsend[i, :, pl.ds(hf * wide, wide)] = product(source, hf).astype(bf16)
+            if i == 0:
+                h_copy(hf, 0).start()
+                h_copy(hf, 1).start()
+            else:
+                h_copy(hf, 1 + i).start()
+
+    def h_relay(hf):
+        for i in range(2):
+            h_copy(hf, i).wait_recv()
+            at = quart(hf, i)
+            hsend[1 + i, :, at] = (
+                hsend[1 + i, :, at].astype(f32) + hrecv[hf, i].astype(f32)
+            ).astype(bf16)
+            h_copy(hf, 4 + i).start()
+
+    h_relay(0)
+    f_copy(x, 1 - k).wait_recv()
+    wholes = [product(x, 0), product(x, 1)]
+    h_relay(1)
     totals("wait")
     exchange(n, me, st_send, st_recv, sem_s.at[0], sem_s.at[1], "wait")
-    size = width // heads
-    scan_states(n, me, st_recv, back_send, tot_ref, size, False)
+    scan_states(n, me, st_recv, back_send, tot_ref, size, 0, False)
     exchange(n, me, back_send, before_ref, sem_b.at[0], sem_b.at[1], "start")
     before_ref[me] = back_send[me]
 
-    def x_at(d):
-        return lax.rem(x + d, nx)
-
-    def product(source):
-        total = jnp.zeros((tok, width), f32)
-        for b in range(nz):
-            total = total + mm(xa[source, b // (nz // 2), b % (nz // 2)], w[b], 0, 0)
-        return total
-
-    def h_copy(d):
-        return remote(
-            hsend.at[d - 1],
-            hrecv.at[d - 1],
-            hsem.at[0, d - 1],
-            hsem.at[1, d - 1],
-            "ctx",
-            x_at(d) * nz + z,
-        )
-
-    order = [1, nx - 1] + list(range(2, nx - 1))
-    for d in order:
-        source = x_at(d)
-        x_copy(x, source).wait_recv()
-        f_copy(source, k).start()
-    w_landed(3)
-    for d in order:
-        source = x_at(d)
-        f_copy(source, 1 - k).wait_recv()
-        hsend[d - 1] = product(source).astype(bf16)
-        h_copy(d).start()
-    f_copy(x, 1 - k).wait_recv()
-    whole = product(x)
-    for d in order:
-        h_copy(d).wait_recv()
-        whole = whole + hrecv[d - 1].astype(f32)
-
-    grad = whole.astype(bf16)
-    ge = (grad.astype(f32) * er_ref[...]).astype(bf16)
-    gst_send[...] = mm(ge, c_ref[...], 0, 0).astype(bf16).reshape(gst_send.shape)
-    exchange(n, me, gst_send, gst_recv, gsem_s.at[0], gsem_s.at[1], "start")
-    gst_recv[me] = gst_send[me]
-
     weights = jnp.zeros((tok, tok), f32)
-    for h in range(heads):
-        gh = grad[:, h * size : (h + 1) * size]
-        uh = u_ref[:, h * size : (h + 1) * size]
-        weights = weights + decay_ref[h].astype(f32) * mm(gh, uh, 1, 1)
-        intra[:, h * size : (h + 1) * size] = mm(mix_ref[h], gh, 0, 0)
+    some = heads // 2
+    weighted = []
+    for hf in range(2):
+        for i in range(2, 6):
+            h_copy(hf, i).wait_recv()
+        grad = (
+            wholes[hf]
+            + jnp.concatenate(
+                [
+                    hrecv[hf, 4].astype(f32) + hrecv[hf, 3].astype(f32),
+                    hrecv[hf, 2].astype(f32) + hrecv[hf, 5].astype(f32),
+                ],
+                axis=1,
+            )
+        ).astype(bf16)
+        ge = (grad.astype(f32) * er_ref[:, hf * wide : (hf + 1) * wide]).astype(bf16)
+        weighted.append(ge)
+        gst_send[hf] = mm(ge, c_ref[...], 0, 0).astype(bf16).reshape(gst_send.shape[1:])
+        exchange(
+            n, me, gst_send.at[hf], gst_recv.at[hf], gsem_s.at[0, hf], gsem_s.at[1, hf], "start"
+        )
+        gst_recv[hf, me] = gst_send[hf, me]
+        for j in range(some):
+            h = hf * some + j
+            gh = grad[:, j * size : (j + 1) * size]
+            uh = u_ref[:, h * size : (h + 1) * size]
+            weights = weights + decay_ref[h].astype(f32) * mm(gh, uh, 1, 1)
+            intra[:, h * size : (h + 1) * size] = mm(mix_ref[h], gh, 0, 0)
     weights = weights.astype(bf16)
     state = b_ref.shape[1]
 
-    exchange(n, me, gst_send, gst_recv, gsem_s.at[0], gsem_s.at[1], "wait")
-    scan_states(n, me, gst_recv, gback_send, tot_ref, size, True)
-    exchange(n, me, gback_send, after, gsem_b.at[0], gsem_b.at[1], "start")
-    after[me] = gback_send[me]
+    for hf in range(2):
+        exchange(
+            n, me, gst_send.at[hf], gst_recv.at[hf], gsem_s.at[0, hf], gsem_s.at[1, hf], "wait"
+        )
+        scan_states(
+            n, me, gst_recv.at[hf], gback_send.at[hf], tot_ref, size, hf * some, True
+        )
+        exchange(
+            n, me, gback_send.at[hf], after.at[hf], gsem_b.at[0, hf], gsem_b.at[1, hf], "start"
+        )
+        after[hf, me] = gback_send[hf, me]
 
     exchange(n, me, back_send, before_ref, sem_b.at[0], sem_b.at[1], "wait")
-    out_map_ref[...] = mm(weights, b_ref[...]) + mm(ge, before_ref[...].reshape(-1, state))
+    before = before_ref[...].reshape(-1, state)
+    out_map_ref[...] = (
+        mm(weights, b_ref[...])
+        + mm(weighted[0], before[0 : some * size])
+        + mm(weighted[1], before[some * size :])
+    )
     in_part = mm(weights, c_ref[...], 0, 0)
 
     def settle(s, _):
         for p in range(3):
             pair_copy(s, p).wait_send()
+        for i in range(6):
+            sum_copy(s, i).wait_send()
+        for i in range(4):
+            grad_copy(s, i, y).wait_send()
         for i in range(3):
-            sum_copy(s, i).wait_send()
-            grad_copy(s, i, y).wait_send()
             fwd_copy(s, i, k, froms[i]).wait_send()
         fwd_copy(s, 3, k, y).wait_send()
         return 0
 
-    lax.fori_loop(0, nx, settle, 0)
-
-    def sent(i, _):
-        dx, dz = i // nz, lax.rem(i, nz)
-        it = ahead(dx, dz)
-        remote(
-            send.at[it], inbuf.at[dx, dz], isem.at[0, i], isem.at[1, i], "ctx", it
-        ).wait_send()
-        remote(eg.at[dx, dz], ret.at[it], rsem.at[0, i], rsem.at[1, i], "ctx", it).wait_send()
-        return 0
-
-    lax.fori_loop(1, n, sent, 0)
+    lax.fori_loop(0, stages, settle, 0)
+
+    each(lambda a, b: in_copy(a, b).wait_send())
+    each(lambda a, b: back_copy(a, b).wait_send())
     for j in range(nz // 2):
         w_copy(j, True).wait_send()
         w_copy(j, False).wait_send()
-    for i in range(3):
+    for i in range(4):
         y_copy(i, y).wait_send()
     for d in order:
         x_copy(x_at(d), x).wait_send()
-        h_copy(d).wait_send()
+    for hf in range(2):
+        for i in range(6):
+            h_copy(hf, i).wait_send()
     for d in range(nx):
         f_copy(x_at(d), k).wait_send()
 
-    exchange(n, me, gback_send, after, gsem_b.at[0], gsem_b.at[1], "wait")
-    later = after[...].reshape(-1, state)
-    in_ref[...] = in_part + mm(ut_ref[...], later)
-    scan_ref[...] = (intra[...] + tail_ref[...] * mm(b_ref[...], later, 1, 1)).astype(bf16)
+    for hf in range(2):
+        exchange(
+            n, me, gback_send.at[hf], after.at[hf], gsem_b.at[0, hf], gsem_b.at[1, hf], "wait"
+        )
+        later = after[hf].reshape(-1, state)
+        at = pl.ds(hf * wide, wide)
+        in_part = in_part + mm(ut_ref[:, at], later)
+        scan_ref[:, at] = (
+            intra[:, at] + tail_ref[:, at] * mm(b_ref[...], later, 1, 1)
+        ).astype(bf16)
+    in_ref[...] = in_part
 
 
 def layer(
@@ -642,8 +806,10 @@
     part = width // n
     cut = cols // 128 * 128
     full = cut + 128
-    rows = nz * cap
+    per, stages = 2 * nx, nz // 2
+    rows = per * cap
     small = jax.ShapeDtypeStruct((tok, state), f32)
+    halves = pltpu.VMEM((2, n, part // 2, state), bf16)
     states = pltpu.VMEM((n, part, state), bf16)
     pairs = DMA((2, n))
     return pl.pallas_call(
@@ -654,9 +820,18 @@
             small,
             small,
         ),
-        in_specs=[VMEM] * 9 + [ANY] * 4,
+        in_specs=[HBM] * 13,
         out_specs=[VMEM] * 4,
         scratch_shapes=[
+            pltpu.VMEM((cols, tok), bf16),
+            pltpu.VMEM((cols, tok), bf16),
+            pltpu.VMEM(ids_t.shape, i32),
+            pltpu.VMEM(prob_t.shape, f32),
+            pltpu.VMEM(counts.shape, i32),
+            pltpu.VMEM((tok, width), bf16),
+            pltpu.VMEM((tok, state), bf16),
+            pltpu.VMEM((tok, state), bf16),
+            pltpu.VMEM(log_t.shape, f32),
             pltpu.VMEM((tok, width), f32),
             pltpu.VMEM((tok, width), f32),
             pltpu.VMEM((tok, width), bf16),
@@ -668,12 +843,12 @@
             pltpu.VMEM((full, hidden), bf16),
             pltpu.VMEM((full, hidden), bf16),
             pltpu.VMEM((n, cap, 2 * cut + 128), bf16),
-            pltpu.VMEM((nx, nz, cap, 2 * cut + 128), bf16),
-            pltpu.VMEM((nx, 3, rows, hidden), bf16),
-            pltpu.VMEM((nx, 3, rows // 2, hidden), bf16),
-            pltpu.VMEM((nx, 3, 3, cap, hidden), bf16),
-            pltpu.VMEM((nx, rows, 2 * hidden), bf16),
-            pltpu.VMEM((nx, nz, cap, cols), bf16),
+            pltpu.VMEM((stages, per, cap, 2 * cut + 128), bf16),
+            pltpu.VMEM((stages, 3, rows, hidden), bf16),
+            pltpu.VMEM((stages, 3, rows // 2, hidden), bf16),
+            pltpu.VMEM((stages, 8, 3, cap, hidden // 2), bf16),
+            pltpu.VMEM((stages, rows, 2 * hidden), bf16),
+            pltpu.VMEM((stages, per, cap, cols), bf16),
             pltpu.VMEM((n, cap, cols), bf16),
             pltpu.VMEM((experts * cap, tok), bf16),
             states,
@@ -683,34 +858,35 @@
             pltpu.VMEM((nz, w.shape[0], width), bf16),
             pltpu.VMEM((ny, nz // 2, w.shape[0], tok), bf16),
             pltpu.VMEM((nx, 2, nz // 2, w.shape[0], tok), bf16),
-            pltpu.VMEM((nx - 1, tok, width), bf16),
-            pltpu.VMEM((nx - 1, tok, width), bf16),
+            pltpu.VMEM((3, tok, width), bf16),
+            pltpu.VMEM((2, 6, tok, width // 4), bf16),
             pltpu.VMEM((tok, width), f32),
-            states,
-            states,
-            states,
-            states,
+            halves,
+            halves,
+            halves,
+            halves,
             DMA((5,)),
             pairs,
-            DMA((2, nx, 3)),
-            DMA((2, nx, 3)),
-            DMA((2, nx, 3)),
-            DMA((2, nx, 4)),
+            DMA((2, stages, 3)),
+            DMA((2, stages, 6)),
+            DMA((2, stages, 4)),
+            DMA((2, stages, 4)),
             pairs,
             pairs,
             pairs,
             pairs,
             DMA((2, nz // 2)),
             DMA((2, nz // 2)),
-            DMA((2, 3)),
+            DMA((2, 4)),
             DMA((2, nx)),
             DMA((2, nx)),
-            DMA((2, nx - 1)),
-            pairs,
-            pairs,
+            DMA((2, 2, 6)),
+            DMA((2, 2, n)),
+            DMA((2, 2, n)),
+            DMA((9,)),
         ],
         compiler_params=pltpu.CompilerParams(
-            collective_id=0, has_side_effects=True, vmem_limit_bytes=46 * 2**20
+            collective_id=0, has_side_effects=True, vmem_limit_bytes=56 * 2**20
         ),
         name="layer",
     )(moe_t, grad_t, ids_t, prob_t, counts, ssd_input, in_map, out_map, log_t, wg, wu, wd, w)

time: 195 us -> 169 us (0.87)
  Pallas kernels: 178 us -> 160 us
  local copies, waits for them, and re-layouts: 14.1 us -> 6.24 us
    pallas_call x1, Pallas kernels: 178 us -> 160 us  [layer(): pl.pallas_call(functools.partial(layer_kernel, nx, nz, ny), out_shape=(ja...]
    unnamed x28 -> x4, local copies, waits for them, and re-layouts: 14.1 us -> 6.24 us
where the time goes in v3:
time: 169 us; the launch traced here: 167 us
  Pallas kernels  160 us (95%)
  local copies, waits for them, and re-layouts  6.24 us (4%)
    pallas_call x1, Pallas kernels, layer(): pl.pallas_call(functools.partial(layer_kernel, nx, nz, ny), out_shape=(ja...  160 us
    unnamed x4, local copies, waits for them, and re-layouts  6.24 us

profile of v3, /device:TPU:1, one launch (start us, length us, event | category | flops | bytes accessed | tf_op | source)
XLA Modules:
  0.0 167.2 jit_solution(14996415028098683711)
XLA Ops:
  0.6 160.3 %layer.1 = (bf16[800,128]{1,0:T(8,128)(2,1)}, bf16[128,1024]{1,0:T(8,128)(2,1)}, f32[128,128]{1,0:T(8,128)}, f32[128,128]{1,0:T(8,128)}) custom-call(bf16[800,128]{1,0:T(8,128)(2,1)} %bitcast.15, bf16[800,128]{1,0:T(8,128)(2,1)} %bitcast.16, s32[2,128]{1,0:T(2,128)} %bitcast.18, f32[2,128]{1,0:T(2,128)} %bitcast.19, s32[1,32]{1,0:T(1,128)} %counts_hbm.1, ...), custom_call_target="tpu_custom_call" | custom-call | tf_op jit(solution)/shard_map/layer/pallas_call | solution.py:815
  160.9 1.6 copy.21
  162.6 1.7 copy.22
  164.2 1.5 copy.23
  165.7 1.5 copy.24

commit v4 on v3

--- a/solution.py
+++ b/solution.py
@@ -50,16 +50,23 @@
         pl.semaphore_signal(barrier, inc=1, device_id={"tp": place}, device_id_type=MESH)
 
 
-def exchange(n, me, src, dst, send, recv, act):
+def exchange(n, me, src, dst, sems, act):
+    if act == "wait":
+        copy = remote(
+            src.at[pl.ds(0, n - 1)],
+            dst.at[pl.ds(0, n - 1)],
+            sems.at[0],
+            sems.at[1],
+            "ctx",
+            lax.rem(me + 1, n),
+        )
+        copy.wait_recv()
+        copy.wait_send()
+        return
+
     def one(i, _):
         to = lax.rem(me + i, n)
-        back = lax.rem(me - i + n, n)
-        if act == "start":
-            remote(src.at[to], dst.at[me], send.at[i], recv.at[i], "ctx", to).start()
-        else:
-            copy = remote(src.at[to], dst.at[back], send.at[i], recv.at[i], "ctx", to)
-            copy.wait_recv()
-            copy.wait_send()
+        remote(src.at[to], dst.at[me], sems.at[0], sems.at[1], "ctx", to).start()
         return 0
 
     lax.fori_loop(1, n, one, 0)
@@ -265,31 +272,30 @@
     mid = w.shape[2] // 2
     last_hop = nz // 2 - 1
 
-    def w_copy(j, upward):
+    def w_part(hf, j, block, upward):
+        if j < last_hop:
+            return w.at[block, :, pl.ds(hf * mid, mid)]
+        return w.at[block, :, pl.ds(hf * mid + (0 if upward else mid // 2), mid // 2)]
+
+    def w_copy(hf, j, upward):
         if upward:
             block, to, sem = lax.rem(z - j + nz, nz), ahead(0, 1), usem
         else:
             block, to, sem = lax.rem(z + j, nz), behind(0, 1), dsem
-        if j < last_hop:
-            at = w.at[block]
-        else:
-            at = w.at[block, :, pl.ds(0 if upward else mid, mid)]
-        return remote(at, at, sem.at[0, j], sem.at[1, j], "ctx", to)
-
-    def w_landed(j):
+        at = w_part(hf, j, block, upward)
+        return remote(at, at, sem.at[0, hf, j], sem.at[1, hf, j], "ctx", to)
+
+    def w_landed(hf, j):
         for upward, sem in ((True, usem), (False, dsem)):
             block = lax.rem(z - j - 1 + nz, nz) if upward else lax.rem(z + j + 1, nz)
-            if j < last_hop:
-                at = w.at[block]
-            else:
-                at = w.at[block, :, pl.ds(0 if upward else mid, mid)]
-            remote(at, at, sem.at[0, j], sem.at[1, j], "ctx", ahead(0, 1)).wait_recv()
-
-    def w_hop(j):
+            at = w_part(hf, j, block, upward)
+            remote(at, at, sem.at[0, hf, j], sem.at[1, hf, j], "ctx", ahead(0, 1)).wait_recv()
+
+    def w_hop(hf, j):
         if j:
-            w_landed(j - 1)
-        w_copy(j, True).start()
-        w_copy(j, False).start()
+            w_landed(hf, j - 1)
+        w_copy(hf, j, True).start()
+        w_copy(hf, j, False).start()
 
     for load in small[2:]:
         load.wait()
@@ -310,10 +316,8 @@
 
     def in_copy(s, j):
         to = target(s, j)
-        at = s * per + j
-        return remote(
-            send.at[to], inbuf.at[s, j], isem.at[0, at], isem.at[1, at], "ctx", to
-        )
+        at = 2 * s + j // (per // 2)
+        return remote(send.at[to], inbuf.at[s, j], isem.at[2 * stages], isem.at[at], "ctx", to)
 
     def post(i, _):
         s, j = i // per, lax.rem(i, per)
@@ -339,32 +343,12 @@
     ut = (u_ref[...].astype(f32) * tail_x).astype(bf16)
     ut_ref[...] = ut
     st_send[...] = mm(ut, b_ref[...], 0, 0).astype(bf16).reshape(st_send.shape)
-    tot_send[...] = jnp.concatenate(
-        [
-            jnp.broadcast_to(total, (tot_send.shape[0], heads)),
-            jnp.zeros((tot_send.shape[0], tot_send.shape[1] - heads), f32),
-        ],
-        axis=1,
-    )
-
-    def totals(act):
-        def one(i, _):
-            to = lax.rem(me + i, n)
-            back = lax.rem(me - i + n, n)
-            if act == "start":
-                remote(
-                    tot_send, tot_ref.at[me], sem_t.at[0, i], sem_t.at[1, i], "ctx", to
-                ).start()
-            else:
-                copy = remote(
-                    tot_send, tot_ref.at[back], sem_t.at[0, i], sem_t.at[1, i], "ctx", to
-                )
-                copy.wait_recv()
-                copy.wait_send()
-            return 0
-
-        lax.fori_loop(1, n, one, 0)
-
+    tot_send[...] = jnp.broadcast_to(
+        jnp.concatenate([total, jnp.zeros((1, tot_send.shape[2] - heads), f32)], axis=1)[None],
+        tot_send.shape,
+    )
+    exchange(n, me, tot_send, tot_ref, sem_t, "start")
+    tot_ref[me] = tot_send[me]
 
     wg[pl.ds(cols, 128 - rest), :] = jnp.zeros((128 - rest, hidden), bf16)
     wu[pl.ds(cols, 128 - rest), :] = jnp.zeros((128 - rest, hidden), bf16)
@@ -428,19 +412,31 @@
         at = grads_at(s, core, dz)
         return remote(at, at, fsem.at[0, s, i], fsem.at[1, s, i], "tp", sib)
 
+    def landed(s, part_at, lo, count):
+        remote(
+            send.at[pl.ds(0, count)],
+            inbuf.at[s, pl.ds(lo, count)],
+            isem.at[2 * stages],
+            isem.at[2 * s + part_at],
+            "ctx",
+            ahead(0, 1),
+        ).wait_recv()
+
     def first(s):
-        def one(i, _):
-            @pl.when(jnp.logical_and(i == per // 2, jnp.logical_and(s != 1, s + 1 < stages)))
-            def _():
-                lax.fori_loop((s + 1) * per, (s + 2) * per, post, 0)
-
-            @pl.when(s * per + i != own[0] * per + own[1])
-            def _():
-                in_copy(s, i).wait_recv()
-
-            return 0
-
-        lax.fori_loop(0, per, one, 0)
+        landed(s, 0, 0, nx)
+
+        @pl.when(jnp.logical_and(s != 1, s + 1 < stages))
+        def _():
+            lax.fori_loop((s + 1) * per, (s + 2) * per, post, 0)
+
+        @pl.when(s < stages - 1)
+        def _():
+            landed(s, 1, nx, nx)
+
+        @pl.when(s == stages - 1)
+        def _():
+            landed(s, 1, nx + 1, nx - 1)
+
         rows = inbuf[s].reshape(per * cap, 2 * cut + 128)
         lasts = rows[:, 2 * cut :]
         for p, w in enumerate((wg, wu, wd)):
@@ -513,14 +509,7 @@
         lax.fori_loop(0, per, one, 0)
 
     def back_copy(s, i):
-        at = s * per + i
-        return remote(
-            eg.at[s, i], ret.at[me], rsem.at[0, at], rsem.at[1, at], "ctx", origin(s, i)
-        )
-
-    def back_landed(s, i):
-        at, it = s * per + i, target(s, i)
-        return remote(eg.at[s, i], ret.at[it], rsem.at[0, at], rsem.at[1, at], "ctx", it)
+        return remote(eg.at[s, i], ret.at[me], rsem.at[0], rsem.at[1], "ctx", origin(s, i))
 
     def stage(s, _):
         second(s)
@@ -549,11 +538,12 @@
 
         @pl.when(s == stages - 2)
         def _():
-            w_hop(0)
+            w_hop(0, 0)
 
         @pl.when(s == stages - 1)
         def _():
             fifth(s - 1)
+            w_hop(0, 1)
 
         third(s)
         return 0
@@ -562,23 +552,17 @@
     first(0)
     lax.fori_loop(0, stages, stage, 0)
     fourth(stages - 1)
-    w_hop(1)
     gathered(stages - 1)
     fifth(stages - 1)
+    w_hop(0, 2)
+    w_hop(1, 0)
     ret[me] = eg[own]
 
-    def each(act):
-        def one(i, _):
-            @pl.when(i != own[0] * per + own[1])
-            def _():
-                act(i // per, lax.rem(i, per))
-
-            return 0
-
-        lax.fori_loop(0, n, one, 0)
-
-    each(lambda a, b: back_landed(a, b).wait_recv())
-    w_hop(2)
+    others = pl.ds(0, n - 1)
+    returned = remote(
+        ret.at[others], ret.at[others], rsem.at[0], rsem.at[1], "ctx", ahead(0, 1)
+    )
+    returned.wait_recv()
     entries = ret[...].reshape(slots, cols)
     input_grad = g_ref[...].astype(f32) + mm(entries, pick[...], 0, 0)
     ya[y] = input_grad.reshape(nz // 2, cols // (nz // 2), tok).astype(bf16)
@@ -621,6 +605,8 @@
         y_copy(i, froms[i]).wait_recv()
         y_copy(2 + i, froms[i]).start()
         pass_on(froms[i])
+    w_hop(0, 3)
+    w_hop(1, 1)
     for i in range(2):
         y_copy(2 + i, y_op).wait_recv()
     pass_on(y_op)
@@ -654,18 +640,15 @@
         )
 
     order = [2, 1, nx - 1]
-    w_hop(3)
+    w_hop(1, 2)
     for d in order:
         source = x_at(d)
         x_copy(x, source).wait_recv()
         f_copy(source, k).start()
-    totals("start")
-    exchange(n, me, st_send, st_recv, sem_s.at[0], sem_s.at[1], "start")
-    st_recv[me] = st_send[me]
-    tot_ref[me] = tot_send[...]
     size = width // heads
-    w_landed(3)
-    for hf in range(2):
+
+    def h_send(hf):
+        w_landed(hf, 3)
         for i, d in enumerate(order):
             source = x_at(d)
             if hf == 0:
@@ -686,15 +669,14 @@
             ).astype(bf16)
             h_copy(hf, 4 + i).start()
 
+    h_send(0)
+    w_hop(1, 3)
+    exchange(n, me, st_send, st_recv, sem_s, "start")
+    st_recv[me] = st_send[me]
     h_relay(0)
     f_copy(x, 1 - k).wait_recv()
-    wholes = [product(x, 0), product(x, 1)]
-    h_relay(1)
-    totals("wait")
-    exchange(n, me, st_send, st_recv, sem_s.at[0], sem_s.at[1], "wait")
-    scan_states(n, me, st_recv, back_send, tot_ref, size, 0, False)
-    exchange(n, me, back_send, before_ref, sem_b.at[0], sem_b.at[1], "start")
-    before_ref[me] = back_send[me]
+    wholes = [product(x, 0)]
+    h_send(1)
 
     weights = jnp.zeros((tok, tok), f32)
     some = heads // 2
@@ -715,32 +697,35 @@
         ge = (grad.astype(f32) * er_ref[:, hf * wide : (hf + 1) * wide]).astype(bf16)
         weighted.append(ge)
         gst_send[hf] = mm(ge, c_ref[...], 0, 0).astype(bf16).reshape(gst_send.shape[1:])
-        exchange(
-            n, me, gst_send.at[hf], gst_recv.at[hf], gsem_s.at[0, hf], gsem_s.at[1, hf], "start"
-        )
+        exchange(n, me, gst_send.at[hf], gst_recv.at[hf], gsem_s.at[hf], "start")
         gst_recv[hf, me] = gst_send[hf, me]
+        if hf == 0:
+            h_relay(1)
+            wholes.append(product(x, 1))
         for j in range(some):
             h = hf * some + j
             gh = grad[:, j * size : (j + 1) * size]
             uh = u_ref[:, h * size : (h + 1) * size]
             weights = weights + decay_ref[h].astype(f32) * mm(gh, uh, 1, 1)
             intra[:, h * size : (h + 1) * size] = mm(mix_ref[h], gh, 0, 0)
+    exchange(n, me, tot_send, tot_ref, sem_t, "wait")
+    exchange(n, me, st_send, st_recv, sem_s, "wait")
+    scan_states(n, me, st_recv, back_send, tot_ref, size, 0, False)
+    exchange(n, me, back_send, before_ref, sem_b, "start")
+    before_ref[me] = back_send[me]
+
     weights = weights.astype(bf16)
     state = b_ref.shape[1]
 
     for hf in range(2):
-        exchange(
-            n, me, gst_send.at[hf], gst_recv.at[hf], gsem_s.at[0, hf], gsem_s.at[1, hf], "wait"
-        )
+        exchange(n, me, gst_send.at[hf], gst_recv.at[hf], gsem_s.at[hf], "wait")
         scan_states(
             n, me, gst_recv.at[hf], gback_send.at[hf], tot_ref, size, hf * some, True
         )
-        exchange(
-            n, me, gback_send.at[hf], after.at[hf], gsem_b.at[0, hf], gsem_b.at[1, hf], "start"
-        )
+        exchange(n, me, gback_send.at[hf], after.at[hf], gsem_b.at[hf], "start")
         after[hf, me] = gback_send[hf, me]
 
-    exchange(n, me, back_send, before_ref, sem_b.at[0], sem_b.at[1], "wait")
+    exchange(n, me, back_send, before_ref, sem_b, "wait")
     before = before_ref[...].reshape(-1, state)
     out_map_ref[...] = (
         mm(weights, b_ref[...])
@@ -763,11 +748,19 @@
 
     lax.fori_loop(0, stages, settle, 0)
 
-    each(lambda a, b: in_copy(a, b).wait_send())
-    each(lambda a, b: back_copy(a, b).wait_send())
-    for j in range(nz // 2):
-        w_copy(j, True).wait_send()
-        w_copy(j, False).wait_send()
+    remote(
+        send.at[others],
+        send.at[others],
+        isem.at[2 * stages],
+        isem.at[0],
+        "ctx",
+        ahead(0, 1),
+    ).wait_send()
+    returned.wait_send()
+    for hf in range(2):
+        for j in range(nz // 2):
+            w_copy(hf, j, True).wait_send()
+            w_copy(hf, j, False).wait_send()
     for i in range(4):
         y_copy(i, y).wait_send()
     for d in order:
@@ -779,9 +772,7 @@
         f_copy(x_at(d), k).wait_send()
 
     for hf in range(2):
-        exchange(
-            n, me, gback_send.at[hf], after.at[hf], gsem_b.at[0, hf], gsem_b.at[1, hf], "wait"
-        )
+        exchange(n, me, gback_send.at[hf], after.at[hf], gsem_b.at[hf], "wait")
         later = after[hf].reshape(-1, state)
         at = pl.ds(hf * wide, wide)
         in_part = in_part + mm(ut_ref[:, at], later)
@@ -811,7 +802,7 @@
     small = jax.ShapeDtypeStruct((tok, state), f32)
     halves = pltpu.VMEM((2, n, part // 2, state), bf16)
     states = pltpu.VMEM((n, part, state), bf16)
-    pairs = DMA((2, n))
+    pair = DMA((2,))
     return pl.pallas_call(
         functools.partial(layer_kernel, nx, nz, ny),
         out_shape=(
@@ -838,7 +829,7 @@
             pltpu.VMEM((heads, tok, tok), bf16),
             pltpu.VMEM((heads, tok, tok), bf16),
             states,
-            pltpu.VMEM((n, 8, 128), f32),
+            pltpu.VMEM((n, 1, 128), f32),
             pltpu.VMEM((full, hidden), bf16),
             pltpu.VMEM((full, hidden), bf16),
             pltpu.VMEM((full, hidden), bf16),
@@ -854,7 +845,7 @@
             states,
             states,
             states,
-            pltpu.VMEM((8, 128), f32),
+            pltpu.VMEM((n, 1, 128), f32),
             pltpu.VMEM((nz, w.shape[0], width), bf16),
             pltpu.VMEM((ny, nz // 2, w.shape[0], tok), bf16),
             pltpu.VMEM((nx, 2, nz // 2, w.shape[0], tok), bf16),
@@ -866,23 +857,23 @@
             halves,
             halves,
             DMA((5,)),
-            pairs,
+            DMA((2 * stages + 1,)),
             DMA((2, stages, 3)),
             DMA((2, stages, 6)),
             DMA((2, stages, 4)),
             DMA((2, stages, 4)),
-            pairs,
-            pairs,
-            pairs,
-            pairs,
-            DMA((2, nz // 2)),
-            DMA((2, nz // 2)),
+            pair,
+            pair,
+            pair,
+            pair,
+            DMA((2, 2, nz // 2)),
+            DMA((2, 2, nz // 2)),
             DMA((2, 4)),
             DMA((2, nx)),
             DMA((2, nx)),
             DMA((2, 2, 6)),
-            DMA((2, 2, n)),
-            DMA((2, 2, n)),
+            DMA((2, 2)),
+            DMA((2, 2)),
             DMA((9,)),
         ],
         compiler_params=pltpu.CompilerParams(
@@ -890,6 +881,32 @@
         ),
         name="layer",
     )(moe_t, grad_t, ids_t, prob_t, counts, ssd_input, in_map, out_map, log_t, wg, wu, wd, w)
+
+
+def keep_kernel(*refs):
+    count = (len(refs) - 1) // 3
+    given, kept, held, sems = refs[:count], refs[count : 2 * count], refs[2 * count : -1], refs[-1]
+    loads = [pltpu.make_async_copy(a, b, sems.at[0, i]) for i, (a, b) in enumerate(zip(given, held))]
+    stores = [pltpu.make_async_copy(a, b, sems.at[1, i]) for i, (a, b) in enumerate(zip(held, kept))]
+    for load in loads:
+        load.start()
+    for load, store in zip(loads, stores):
+        load.wait()
+        store.start()
+    for store in stores:
+        store.wait()
+
+
+def keep(arrays):
+    return pl.pallas_call(
+        keep_kernel,
+        out_shape=tuple(jax.ShapeDtypeStruct(a.shape, a.dtype) for a in arrays),
+        in_specs=[HBM] * len(arrays),
+        out_specs=[HBM] * len(arrays),
+        scratch_shapes=[pltpu.VMEM(a.shape, a.dtype) for a in arrays] + [DMA((2, len(arrays)))],
+        compiler_params=pltpu.CompilerParams(vmem_limit_bytes=60 * 2**20),
+        name="keep",
+    )(*arrays)
 
 
 def body(
@@ -911,7 +928,7 @@
     ny = lax.axis_size("tp") // 2
     nx = ny
     nz = n // nx
-    grad_t, scan_grad, in_map_grad, out_map_grad = layer(
+    outs = layer(
         (nx, nz, ny),
         moe_input.T,
         out_grad.T,
@@ -927,6 +944,7 @@
         w_down[0].T,
         out_weight,
     )
+    grad_t, scan_grad, in_map_grad, out_map_grad = keep(outs)
     return (grad_t.T, scan_grad, in_map_grad, out_map_grad)
 
 

time: 169 us -> 155 us (0.917)
  Pallas kernels: 160 us -> 153 us
  local copies, waits for them, and re-layouts: 6.24 us -> 0 us
    pallas_call x1, Pallas kernels: 160 us -> 151 us  [layer(): pl.pallas_call(functools.partial(layer_kernel, nx, nz, ny), out_shape=(ja...]
    unnamed x4 -> x0, local copies, waits for them, and re-layouts: 6.24 us -> none
    pallas_call x0 -> x1, Pallas kernels: none -> 1.87 us  [keep(): pl.pallas_call(keep_kernel, out_shape=tuple((jax.ShapeDtypeStruct(a.shape...]
where the time goes in v4:
time: 155 us; the launch traced here: 154 us
  Pallas kernels  153 us (99%)
    pallas_call x1, Pallas kernels, layer(): pl.pallas_call(functools.partial(layer_kernel, nx, nz, ny), out_shape=(ja...  151 us

profile of v4, /device:TPU:1, one launch (start us, length us, event | category | flops | bytes accessed | tf_op | source)
XLA Modules:
  0.0 153.9 jit_solution(6876351034810658429)
XLA Ops:
  0.6 151.3 %layer.1 = (bf16[800,128]{1,0:T(8,128)(2,1)}, bf16[128,1024]{1,0:T(8,128)(2,1)}, f32[128,128]{1,0:T(8,128)}, f32[128,128]{1,0:T(8,128)}) custom-call(bf16[800,128]{1,0:T(8,128)(2,1)} %bitcast.14, bf16[800,128]{1,0:T(8,128)(2,1)} %bitcast.15, s32[2,128]{1,0:T(2,128)} %bitcast.17, f32[2,128]{1,0:T(2,128)} %bitcast.18, s32[1,32]{1,0:T(1,128)} %counts_hbm.1, ...), custom_call_target="tpu_custom_call" | custom-call | tf_op jit(solution)/shard_map/layer/pallas_call | solution.py:806
  151.9 1.9 %keep.1 = (bf16[800,128]{1,0:T(8,128)(2,1)}, bf16[128,1024]{1,0:T(8,128)(2,1)}, f32[128,128]{1,0:T(8,128)}, f32[128,128]{1,0:T(8,128)}) custom-call(bf16[800,128]{1,0:T(8,128)(2,1)} %get-tuple-element.12.refs_0_, bf16[128,1024]{1,0:T(8,128)(2,1)} %get-tuple-element.13.refs_1_, f32[128,128]{1,0:T(8,128)} %get-tuple-element.14.refs_2_, ...), custom_call_target="tpu_custom_call" | custom-call | tf_op jit(solution)/shard_map/keep/pallas_call | solution.py:901

commit v5 on v4

--- a/solution.py
+++ b/solution.py
@@ -554,8 +554,8 @@
     fourth(stages - 1)
     gathered(stages - 1)
     fifth(stages - 1)
+    w_hop(1, 0)
     w_hop(0, 2)
-    w_hop(1, 0)
     ret[me] = eg[own]
 
     others = pl.ds(0, n - 1)
@@ -568,9 +568,8 @@
     ya[y] = input_grad.reshape(nz // 2, cols // (nz // 2), tok).astype(bf16)
 
     def y_copy(i, dz):
-        at = ya.at[dz]
-        if i >= 2:
-            at = ya.at[dz, pl.ds((i - 2) * (nz // 4), nz // 4)]
+        first_half = (0, 1, 1, 0, 0, 1)[i]
+        at = ya.at[dz, pl.ds(first_half * (nz // 4), nz // 4)]
         return remote(at, at, ysem.at[0, i], ysem.at[1, i], "tp", (up, dn)[i % 2])
 
     def x_copy(place, source):
@@ -597,18 +596,20 @@
             xa[x, k] = ya[place]
             f_copy(x, k).start()
 
-    for i in range(2):
+    for i in range(4):
         y_copy(i, y).start()
     pass_on(y)
     out_ref[...] = input_grad.astype(bf16)
     for i in range(2):
         y_copy(i, froms[i]).wait_recv()
-        y_copy(2 + i, froms[i]).start()
+        y_copy(4 + i, froms[i]).start()
+    w_hop(1, 1)
+    for i in range(2):
+        y_copy(2 + i, froms[i]).wait_recv()
         pass_on(froms[i])
     w_hop(0, 3)
-    w_hop(1, 1)
     for i in range(2):
-        y_copy(2 + i, y_op).wait_recv()
+        y_copy(4 + i, y_op).wait_recv()
     pass_on(y_op)
 
     def x_at(d):
@@ -641,6 +642,8 @@
 
     order = [2, 1, nx - 1]
     w_hop(1, 2)
+    exchange(n, me, st_send, st_recv, sem_s, "start")
+    st_recv[me] = st_send[me]
     for d in order:
         source = x_at(d)
         x_copy(x, source).wait_recv()
@@ -671,11 +674,14 @@
 
     h_send(0)
     w_hop(1, 3)
-    exchange(n, me, st_send, st_recv, sem_s, "start")
-    st_recv[me] = st_send[me]
     h_relay(0)
     f_copy(x, 1 - k).wait_recv()
     wholes = [product(x, 0)]
+    exchange(n, me, tot_send, tot_ref, sem_t, "wait")
+    exchange(n, me, st_send, st_recv, sem_s, "wait")
+    scan_states(n, me, st_recv, back_send, tot_ref, size, 0, False)
+    exchange(n, me, back_send, before_ref, sem_b, "start")
+    before_ref[me] = back_send[me]
     h_send(1)
 
     weights = jnp.zeros((tok, tok), f32)
@@ -708,12 +714,6 @@
             uh = u_ref[:, h * size : (h + 1) * size]
             weights = weights + decay_ref[h].astype(f32) * mm(gh, uh, 1, 1)
             intra[:, h * size : (h + 1) * size] = mm(mix_ref[h], gh, 0, 0)
-    exchange(n, me, tot_send, tot_ref, sem_t, "wait")
-    exchange(n, me, st_send, st_recv, sem_s, "wait")
-    scan_states(n, me, st_recv, back_send, tot_ref, size, 0, False)
-    exchange(n, me, back_send, before_ref, sem_b, "start")
-    before_ref[me] = back_send[me]
-
     weights = weights.astype(bf16)
     state = b_ref.shape[1]
 
@@ -761,7 +761,7 @@
         for j in range(nz // 2):
             w_copy(hf, j, True).wait_send()
             w_copy(hf, j, False).wait_send()
-    for i in range(4):
+    for i in range(6):
         y_copy(i, y).wait_send()
     for d in order:
         x_copy(x_at(d), x).wait_send()
@@ -868,7 +868,7 @@
             pair,
             DMA((2, 2, nz // 2)),
             DMA((2, 2, nz // 2)),
-            DMA((2, 4)),
+            DMA((2, 6)),
             DMA((2, nx)),
             DMA((2, nx)),
             DMA((2, 2, 6)),

time: 155 us -> 153 us (0.987)
  Pallas kernels: 153 us -> 151 us
    pallas_call x1, Pallas kernels: 151 us -> 149 us  [layer(): pl.pallas_call(functools.partial(layer_kernel, nx, nz, ny), out_shape=(ja...]
where the time goes in v5:
time: 153 us; the launch traced here: 152 us
  Pallas kernels  151 us (99%)
    pallas_call x1, Pallas kernels, layer(): pl.pallas_call(functools.partial(layer_kernel, nx, nz, ny), out_shape=(ja...  149 us

profile of v5, /device:TPU:1, one launch (start us, length us, event | category | flops | bytes accessed | tf_op | source)
XLA Modules:
  0.0 151.8 jit_solution(58302685590040759)
XLA Ops:
  0.6 149.1 %layer.1 = (bf16[800,128]{1,0:T(8,128)(2,1)}, bf16[128,1024]{1,0:T(8,128)(2,1)}, f32[128,128]{1,0:T(8,128)}, f32[128,128]{1,0:T(8,128)}) custom-call(bf16[800,128]{1,0:T(8,128)(2,1)} %bitcast.14, bf16[800,128]{1,0:T(8,128)(2,1)} %bitcast.15, s32[2,128]{1,0:T(2,128)} %bitcast.17, f32[2,128]{1,0:T(2,128)} %bitcast.18, s32[1,32]{1,0:T(1,128)} %counts_hbm.1, ...), custom_call_target="tpu_custom_call" | custom-call | tf_op jit(solution)/shard_map/layer/pallas_call | solution.py:806
  149.7 1.9 %keep.1 = (bf16[800,128]{1,0:T(8,128)(2,1)}, bf16[128,1024]{1,0:T(8,128)(2,1)}, f32[128,128]{1,0:T(8,128)}, f32[128,128]{1,0:T(8,128)}) custom-call(bf16[800,128]{1,0:T(8,128)(2,1)} %get-tuple-element.12.refs_0_, bf16[128,1024]{1,0:T(8,128)(2,1)} %get-tuple-element.13.refs_1_, f32[128,128]{1,0:T(8,128)} %get-tuple-element.14.refs_2_, ...), custom_call_target="tpu_custom_call" | custom-call | tf_op jit(solution)/shard_map/keep/pallas_call | solution.py:901

commit v6 on v5

--- a/solution.py
+++ b/solution.py
@@ -174,6 +174,7 @@
     gsem_s,
     gsem_b,
     lsem,
+    osem,
 ):
     n = nx * nz
     me = lax.axis_index("ctx")
@@ -372,8 +373,8 @@
         return remote(
             part.at[s, p, pl.ds(other, half)],
             precv.at[s, p],
-            psem.at[0, s, p],
-            psem.at[1, s, p],
+            osem.at[0],
+            psem.at[s, p],
             "tp",
             sib,
         )
@@ -394,7 +395,7 @@
             rsum.at[s, 7],
         )[i]
         return remote(
-            src, rsum.at[s, i], ssem.at[0, s, i], ssem.at[1, s, i], "tp", (up, dn)[i % 2]
+            src, rsum.at[s, i], osem.at[1], ssem.at[s, i], "tp", (up, dn)[i % 2]
         )
 
     def grads_at(s, core, dz):
@@ -406,11 +407,11 @@
         at = gall.at[s, chunk(dz)]
         if i >= 2:
             at = gall.at[s, chunk(dz), pl.ds((i - 2) * hidden, hidden)]
-        return remote(at, at, gsem.at[0, s, i], gsem.at[1, s, i], "tp", (up, dn)[i % 2])
+        return remote(at, at, osem.at[2], gsem.at[s, i], "tp", (up, dn)[i % 2])
 
     def fwd_copy(s, i, core, dz):
         at = grads_at(s, core, dz)
-        return remote(at, at, fsem.at[0, s, i], fsem.at[1, s, i], "tp", sib)
+        return remote(at, at, osem.at[3], fsem.at[s, i], "tp", sib)
 
     def landed(s, part_at, lo, count):
         remote(
@@ -425,7 +426,7 @@
     def first(s):
         landed(s, 0, 0, nx)
 
-        @pl.when(jnp.logical_and(s != 1, s + 1 < stages))
+        @pl.when(s == 0)
         def _():
             lax.fori_loop((s + 1) * per, (s + 2) * per, post, 0)
 
@@ -531,6 +532,10 @@
         @pl.when(s > 0)
         def _():
             gathered(s - 1)
+
+        @pl.when(s == 1)
+        def _():
+            lax.fori_loop(3 * per, 4 * per, post, 0)
 
         @pl.when(s + 1 < stages)
         def _():
@@ -734,19 +739,15 @@
     )
     in_part = mm(weights, c_ref[...], 0, 0)
 
-    def settle(s, _):
-        for p in range(3):
-            pair_copy(s, p).wait_send()
-        for i in range(6):
-            sum_copy(s, i).wait_send()
-        for i in range(4):
-            grad_copy(s, i, y).wait_send()
-        for i in range(3):
-            fwd_copy(s, i, k, froms[i]).wait_send()
-        fwd_copy(s, 3, k, y).wait_send()
-        return 0
-
-    lax.fori_loop(0, stages, settle, 0)
+    for i, sent in enumerate(
+        (
+            part.at[:, :, pl.ds(other, half)],
+            rsum.at[:, pl.ds(0, 6)],
+            gall.at[:, pl.ds(0, 3 * cap)],
+            gall.at[:, pl.ds(mine, half)],
+        )
+    ):
+        remote(sent, sent, osem.at[i], psem.at[0, 0], "tp", sib).wait_send()
 
     remote(
         send.at[others],
@@ -858,10 +859,10 @@
             halves,
             DMA((5,)),
             DMA((2 * stages + 1,)),
-            DMA((2, stages, 3)),
-            DMA((2, stages, 6)),
-            DMA((2, stages, 4)),
-            DMA((2, stages, 4)),
+            DMA((stages, 3)),
+            DMA((stages, 6)),
+            DMA((stages, 4)),
+            DMA((stages, 4)),
             pair,
             pair,
             pair,
@@ -875,6 +876,7 @@
             DMA((2, 2)),
             DMA((2, 2)),
             DMA((9,)),
+            DMA((4,)),
         ],
         compiler_params=pltpu.CompilerParams(
             collective_id=0, has_side_effects=True, vmem_limit_bytes=56 * 2**20

time: 153 us -> 151 us (0.987)
  Pallas kernels: 151 us -> 149 us
    pallas_call x1, Pallas kernels: 149 us -> 147 us  [layer(): pl.pallas_call(functools.partial(layer_kernel, nx, nz, ny), out_shape=(ja...]
where the time goes in v6:
time: 151 us; the launch traced here: 150 us
  Pallas kernels  149 us (99%)
    pallas_call x1, Pallas kernels, layer(): pl.pallas_call(functools.partial(layer_kernel, nx, nz, ny), out_shape=(ja...  147 us

profile of v6, /device:TPU:1, one launch (start us, length us, event | category | flops | bytes accessed | tf_op | source)
XLA Modules:
  0.0 150.0 jit_solution(17172587444054529427)
XLA Ops:
  0.6 147.4 %layer.1 = (bf16[800,128]{1,0:T(8,128)(2,1)}, bf16[128,1024]{1,0:T(8,128)(2,1)}, f32[128,128]{1,0:T(8,128)}, f32[128,128]{1,0:T(8,128)}) custom-call(bf16[800,128]{1,0:T(8,128)(2,1)} %bitcast.14, bf16[800,128]{1,0:T(8,128)(2,1)} %bitcast.15, s32[2,128]{1,0:T(2,128)} %bitcast.17, f32[2,128]{1,0:T(2,128)} %bitcast.18, s32[1,32]{1,0:T(1,128)} %counts_hbm.1, ...), custom_call_target="tpu_custom_call" | custom-call | tf_op jit(solution)/shard_map/layer/pallas_call | solution.py:807
  148.0 1.9 %keep.1 = (bf16[800,128]{1,0:T(8,128)(2,1)}, bf16[128,1024]{1,0:T(8,128)(2,1)}, f32[128,128]{1,0:T(8,128)}, f32[128,128]{1,0:T(8,128)}) custom-call(bf16[800,128]{1,0:T(8,128)(2,1)} %get-tuple-element.12.refs_0_, bf16[128,1024]{1,0:T(8,128)(2,1)} %get-tuple-element.13.refs_1_, f32[128,128]{1,0:T(8,128)} %get-tuple-element.14.refs_2_, ...), custom_call_target="tpu_custom_call" | custom-call | tf_op jit(solution)/shard_map/keep/pallas_call | solution.py:903
